TPU v7x, 512 devices: a whole 4x4x16 slice. The times are simulated.
512 devices in a mesh: dp: 8 (over z_lo), tm: 16 (over z_hi, x, core), mp: 4 (over y).
Axes of the slice: x: 4, y: 4, z: 16 (z_hi: 2, z_lo: 8; z = z_hi * 8 + z_lo), core: 2. Of those that a mesh axis runs over, the one named last changes fastest.
Arguments:
- waveform: float32 [8, 2621440], P('dp', ('tm', 'mp')), may hold values from -6 to 6
- lengths: int32 [8], P('dp'), may hold values from 327680 to 2621440, as said below
- sub_weight: bfloat16 [896, 1536], P(('dp', 'tm'), 'mp'), may hold values from -0.1875 to 0.1875
- value_weight: bfloat16 [1536, 1536], P(('dp', 'tm'), 'mp'), may hold values from -0.15625 to 0.15625
- gate_weight: bfloat16 [1536, 1536], P(('dp', 'tm'), 'mp'), may hold values from -0.15625 to 0.15625
- out_weight: bfloat16 [1536, 1536], P('mp', ('dp', 'tm')), may hold values from -0.15625 to 0.15625
- depth_kernel: float32 [31, 1536], P(None, 'mp'), may hold values from -1 to 1
- norm_scale: float32 [1536], P('mp'), may hold values from 0.5 to 2
- norm_shift: float32 [1536], P('mp'), may hold values from -3 to 3
Outputs:
- encoded: bfloat16 [8, 4096, 1536], P('dp', 'tm', 'mp')
Inputs may be any that keep to these rules, and one draw needn't show every extreme that they name: `lengths`: in every draw one utterance has exactly 2621440 valid samples.
All inputs are finite; a program needn't handle non-finite values.
Results may differ from a plain program's by a relative error of at most 0.013.
Values may be sent and summed in bfloat16 or wider, within the bound.
A program may use at most 64 MiB of HBM per device.

v0:
```python
import math

import jax
import jax.numpy as jnp
from jax import lax
from jax.sharding import PartitionSpec as P

MEL = 128
WIN = 400
HOP = 160
STRIDE = 4
TAPS = 7
KERNEL = 31
BINS = 201


def shifted_2(block, axis, distance):
    devices = range(lax.axis_size(axis))
    route = [(i - distance, i) for i in devices if i - distance in devices]
    return lax.ppermute(block, axis, route)


def padded_2(shard, sides, width):
    for axis, dim in sides:
        size, length = (lax.axis_size(axis), shard.shape[dim])
        up = [(i, (i + 1) % size) for i in range(size - 1)]
        down = [(j, i) for i, j in up]
        last = lax.slice_in_dim(shard, length - width, length, axis=dim)
        initial = lax.slice_in_dim(shard, 0, width, axis=dim)
        before = lax.ppermute(last, axis, up)
        after = lax.ppermute(initial, axis, down)
        shard = jnp.concatenate([before, shard, after], axis=dim)
    return shard


def mel_filters(bin_count, band_count, frame_width):
    mel_top = 2595.0 * math.log10(1.0 + 8000.0 / 700.0)
    border_list = [
        700.0
        * (10.0 ** (band_index * mel_top / (band_count + 1) / 2595.0) - 1.0)
        * frame_width
        / 16000.0
        for band_index in range(band_count + 2)
    ]
    borders = jnp.asarray(border_list, dtype=jnp.float32)
    centers = jnp.arange(bin_count, dtype=jnp.float32)[:, None]
    middle = borders[1:-1][None, :]
    lower_edge = jnp.minimum(borders[:-2], borders[1:-1] - 1.0)[None, :]
    upper_edge = jnp.maximum(borders[2:], borders[1:-1] + 1.0)[None, :]
    rising = (centers - lower_edge) / (middle - lower_edge)
    falling = (upper_edge - centers) / (upper_edge - middle)
    return jnp.maximum(0.0, jnp.minimum(rising, falling))


def hann_window(width):
    phases = jnp.arange(width, dtype=jnp.float32) * (2.0 * math.pi / width)
    return 0.5 - 0.5 * jnp.cos(phases)


def fourier_table():
    sample_index = lax.broadcasted_iota(jnp.int32, (WIN, BINS), 0)
    bin_index = lax.broadcasted_iota(jnp.int32, (WIN, BINS), 1)
    phases = (sample_index * bin_index % WIN).astype(jnp.float32) * (2.0 * math.pi / WIN)
    return jnp.concatenate([jnp.cos(phases), jnp.sin(phases)], axis=1)


def shards(
    waveform,
    lengths,
    sub_weight,
    value_weight,
    gate_weight,
    out_weight,
    depth_kernel,
    norm_scale,
    norm_shift,
):
    length = lengths[0]
    model_ways = lax.axis_size("mp")
    segment = lax.axis_index("tm") * model_ways + lax.axis_index("mp")
    samples = waveform[0]
    local_count = samples.shape[0]
    mel_local = local_count // HOP
    position = segment * local_count + lax.iota(jnp.int32, local_count)
    masked = jnp.where(position < length, samples, jnp.float32(0.0))
    borrowed = shifted_2(masked[: WIN - HOP], ("tm", "mp"), -1)
    tail_zeros = jnp.zeros((3 * HOP - WIN,), jnp.float32)
    blocks = jnp.concatenate([masked, borrowed, tail_zeros]).reshape(mel_local + 2, HOP)
    frames = jnp.concatenate(
        [blocks[:mel_local], blocks[1 : mel_local + 1], blocks[2 : mel_local + 2, : WIN - 2 * HOP]],
        axis=1,
    )
    windowed = frames * hann_window(WIN)
    spectrum = jnp.dot(windowed, fourier_table(), precision=lax.Precision.HIGHEST)
    power_bins = spectrum[:, :BINS] ** 2 + spectrum[:, BINS:] ** 2
    filters = mel_filters(BINS, MEL, WIN)
    mel_energy = jnp.dot(power_bins, filters, precision=lax.Precision.HIGHEST)
    log_energy = jnp.log(mel_energy + 1e-06)
    valid_mel = (segment * mel_local + lax.iota(jnp.int32, mel_local) < length // HOP)[:, None]
    first_moment = jnp.sum(jnp.where(valid_mel, log_energy, 0.0), axis=0)
    squares = jnp.sum(jnp.where(valid_mel, log_energy * log_energy, 0.0), axis=0)
    first_moment, squares = lax.psum((first_moment, squares), ("tm", "mp"))
    valid_count = (length // HOP).astype(jnp.float32)
    mel_mean = first_moment / valid_count
    mel_var = squares / valid_count - mel_mean * mel_mean
    normed_mel = jnp.where(
        valid_mel, (log_energy - mel_mean) * lax.rsqrt(mel_var + 1e-05), 0.0
    ).astype(jnp.bfloat16)
    gathered = lax.all_gather(normed_mel, "mp", axis=0, tiled=True)
    reach_mel = TAPS // 2
    earlier = shifted_2(gathered[gathered.shape[0] - reach_mel :], "tm", 1)
    padded = jnp.concatenate(
        [earlier, gathered, jnp.zeros((reach_mel, gathered.shape[1]), jnp.bfloat16)], axis=0
    )
    frame_count = gathered.shape[0] // STRIDE
    leading = padded[: STRIDE * frame_count].reshape(frame_count, STRIDE * MEL)
    second = padded[STRIDE : STRIDE * frame_count + STRIDE].reshape(frame_count, STRIDE * MEL)[
        :, : (TAPS - STRIDE) * MEL
    ]
    stacked = jnp.concatenate([leading, second], axis=1)
    width_local = value_weight.shape[1]
    start_sub = jnp.zeros((frame_count, width_local), jnp.float32)
    columns = stacked
    own_features = (
        start_sub
        + jnp.dot(
            columns,
            lax.all_gather(sub_weight, ("dp", "tm"), axis=0, tiled=True),
            preferred_element_type=jnp.float32,
        )
    ).astype(jnp.bfloat16)
    all_features = lax.all_gather(own_features, "mp", axis=1, tiled=True)
    widened = all_features.astype(jnp.float32)
    centered = widened - jnp.mean(widened, axis=1, keepdims=True)
    spread = jnp.mean(centered * centered, axis=1, keepdims=True)
    normed = (centered * lax.rsqrt(spread + 1e-05)).astype(jnp.bfloat16)
    frame_limit = length // (STRIDE * HOP)
    valid_frames = (
        lax.axis_index("tm") * frame_count + lax.iota(jnp.int32, frame_count) < frame_limit
    )[:, None]
    start_glu = jnp.zeros((frame_count, width_local), jnp.float32)
    columns = normed
    value_sum = start_glu + jnp.dot(
        columns,
        lax.all_gather(value_weight, ("dp", "tm"), axis=0, tiled=True),
        preferred_element_type=jnp.float32,
    )
    gate_sum = start_glu + jnp.dot(
        columns,
        lax.all_gather(gate_weight, ("dp", "tm"), axis=0, tiled=True),
        preferred_element_type=jnp.float32,
    )
    gated = jnp.where(valid_frames, value_sum * jax.nn.sigmoid(gate_sum), 0.0).astype(jnp.bfloat16)
    padded_gated = padded_2(gated, (("tm", 0),), KERNEL // 2).astype(jnp.float32)
    depthwise = jnp.zeros((frame_count, width_local), jnp.float32)
    for tap_index in range(KERNEL):
        depthwise = (
            depthwise + depth_kernel[tap_index] * padded_gated[tap_index : tap_index + frame_count]
        )
    shifted = depthwise * norm_scale + norm_shift
    activated = jax.nn.silu(shifted).astype(jnp.bfloat16)
    shard_piece = lax.all_gather(out_weight, ("dp", "tm"), axis=1, tiled=True)
    partial_sums = jnp.dot(activated, shard_piece, preferred_element_type=jnp.float32)
    summed = lax.psum_scatter(
        partial_sums.astype(jnp.bfloat16), "mp", scatter_dimension=1, tiled=True
    ).astype(jnp.float32)
    encoded = jnp.where(valid_frames, own_features.astype(jnp.float32) + summed, 0.0)
    return encoded.astype(jnp.bfloat16)[None]


def solution(mesh):
    placed = (
        P("dp", ("tm", "mp")),
        P("dp"),
        P(("dp", "tm"), "mp"),
        P(("dp", "tm"), "mp"),
        P(("dp", "tm"), "mp"),
        P("mp", ("dp", "tm")),
        P(None, "mp"),
        P("mp"),
        P("mp"),
    )
    return jax.shard_map(
        shards, mesh=mesh, in_specs=placed, out_specs=P("dp", "tm", "mp"), check_vma=False
    )
```

profile of v0, /device:TPU:1, one launch (start us, length us, event | category | flops | bytes accessed | tf_op | source)
XLA Modules:
  0.0 712.9 jit_solution(10681924244531750637)
XLA Ops:
  6.5 0.7 all-gather.8.cloned.1.call-update
  7.3 0.0 all-gather.10.cloned.1.call-start
  7.3 0.7 all-gather.10.cloned.1.call-update
  8.0 0.0 all-gather.12.cloned.1.call-start
  8.7 0.9 fusion.66
  9.7 6.0 collective-permute-start
  15.7 0.0 reduce-scatter.4.cloned.1.call-start
  15.8 1.7 fusion.26
  17.5 0.5 broadcast.139
  18.0 1.8 reduce.65
  19.8 0.1 squeeze.9
  20.0 253.4 %all-gather = bf16[128,7,384]{2,1,0:T(8,128)(2,1)S(1)} all-gather(bf16[1,7,384]{2,1,0:T(8,128)(2,1)S(1)} %bitcast.29), channel_id=1, replica_groups=mesh['dp'=8,'tm'=16,'mp'=4] {'dp','tm'}, dimensions={0}, use_global_device_ids=true | all-gather | bytes 693504 | tf_op jit(solution)/shard_map/all_gather | solution.py:128
  273.4 0.1 slice_reduce_fusion.30
  273.6 0.1 concatenate.26
  273.7 0.1 reshape.56
  273.8 0.1 pad_maximum_fusion.1
  274.0 0.1 slice.244
  274.1 2.1 fusion.11
  276.2 0.7 select_reduce_fusion
  276.9 264.6 %all-reduce.1 = (f32[128]{0:T(128)S(1)}, f32[128]{0:T(128)S(1)}) all-reduce(f32[128]{0:T(128)S(1)} %get-tuple-element.6, f32[128]{0:T(128)S(1)} %get-tuple-element.5), channel_id=1, replica_groups=mesh['dp'=8,'tm'=16,'mp'=4] {'tm','mp'}, use_global_device_ids=true, to_apply=%region_1.2 | all-reduce | flops 256 | bytes 2048 | tf_op jit(solution)/shard_map/psum | solution.py:102
  541.5 0.1 select_convert_fusion.1
  541.6 10.0 %all_gather.18 = bf16[1024,128]{1,0:T(8,128)(2,1)S(1)} all-gather(bf16[256,128]{1,0:T(8,128)(2,1)S(1)} %select_convert_fusion.1), channel_id=1, replica_groups=mesh['dp'=8,'tm'=16,'mp'=4] {'mp'}, dimensions={0}, use_global_device_ids=true | all-gather | bytes 327680 | tf_op jit(solution)/shard_map/all_gather | solution.py:109
  551.6 1.9 collective-permute-start.1
  553.5 0.2 reshape.60
  553.7 26.3 %collective-permute-done.1 = bf16[3,128]{1,0:T(4,128)(2,1)S(1)} collective-permute-done((bf16[3,128]{1,0:T(4,128)(2,1)S(1)}, bf16[3,128]{1,0:T(4,128)(2,1)S(1)}, u32[]{:S(2)}, u32[]{:S(2)}) %collective-permute-start.1) | collective-permute-done | bytes 800 | tf_op jit(solution)/shard_map/ppermute | solution.py:20
  580.0 0.1 pad_maximum_fusion
  580.2 0.2 reshape.58
  580.4 0.2 reshape.57
  580.5 0.4 convolution_convert_fusion.1
  580.9 11.9 %all_gather.20 = bf16[256,1536]{1,0:T(8,128)(2,1)S(1)} all-gather(bf16[256,384]{1,0:T(8,128)(2,1)S(1)} %convolution_convert_fusion.1), channel_id=1, replica_groups=mesh['dp'=8,'tm'=16,'mp'=4] {'mp'}, dimensions={1}, use_global_device_ids=true | all-gather | bytes 983040 | tf_op jit(solution)/shard_map/all_gather | solution.py:132
  592.8 0.2 convert_reduce_fusion
  593.0 0.4 fusion.2
  593.4 0.0 all-gather.8.cloned.1.call-done
  593.4 2.3 reshape.62
  595.7 2.3 reshape.64
  598.0 0.6 fusion.84
  598.6 0.7 fusion.9
  599.3 1.9 collective-permute-start.2
  601.3 4.8 collective-permute-start.3
  606.1 0.1 slice_reduce_fusion.29
  606.1 66.6 %all-gather.12.cloned.1.call-done = bf16[128,12,384]{2,1,0:T(8,128)(2,1)} async-done(((bf16[1,12,384]{2,1,0:T(8,128)(2,1)}), bf16[128,12,384]{2,1,0:T(8,128)(2,1)}) %all-gather.12.cloned.1.call-update) | async-done | bytes 1179664 | tf_op jit(solution)/shard_map/all_gather | solution.py:162
  672.8 2.3 reshape.66
  675.1 0.1 maximum_convert_fusion
  675.1 1.8 convolution_convert_fusion
  676.9 1.2 copy.11
  678.1 26.4 %reduce-scatter.4.cloned.1.call-done = bf16[384,256]{1,0:T(8,128)(2,1)} async-done(((bf16[1536,256]{1,0:T(8,128)(2,1)}), bf16[384,256]{1,0:T(8,128)(2,1)}) %reduce-scatter.4.cloned.1.call-update) | async-done | bytes 196624
  704.5 1.1 copy.12
  705.6 0.8 fusion.65
  (36 shorter events, 0.3 us)
Async XLA Ops:
  6.5 13.5 %copy-start.1 = (bf16[7,384]{1,0:T(8,128)(2,1)S(1)}, bf16[7,384]{1,0:T(8,128)(2,1)}, u32[]{:S(2)}) copy-start(bf16[7,384]{1,0:T(8,128)(2,1)} %param.12) | copy-start | bytes 16132
  6.5 266.8 %copy-start = (f32[31,384]{1,0:T(8,128)S(1)}, f32[31,384]{1,0:T(8,128)}, u32[]{:S(2)}) copy-start(f32[31,384]{1,0:T(8,128)} %param.16) | copy-start | bytes 142852
  6.5 586.9 %all-gather.8.cloned.1.call-start = ((), (), s32[]{:S(2)}) async-start(), calls=%async_computation.1 | async-start | bytes 1585152 | tf_op jit(solution)/shard_map/all_gather | solution.py:145
  7.3 588.4 %all-gather.10.cloned.1.call-start = ((), (), s32[]{:S(2)}) async-start(), calls=%async_computation.2 | async-start | bytes 1585152 | tf_op jit(solution)/shard_map/all_gather | solution.py:150
  8.0 664.8 %all-gather.12.cloned.1.call-start = ((), (), s32[]{:S(2)}) async-start(), calls=%async_computation.3 | async-start | bytes 1585152 | tf_op jit(solution)/shard_map/all_gather | solution.py:162
  9.7 263.9 %collective-permute-start = (f32[240]{0:T(256)S(1)}, f32[240]{0:T(256)S(1)}, u32[]{:S(2)}, u32[]{:S(2)}) collective-permute-start(f32[240]{0:T(256)S(1)} %slice.319), channel_id=1, source_target_pairs={{1,0},{2,1},{3,2},{4,3},{5,4},{6,5},{7,6},{8,7},{9,8},{10,9},{11,1... | collective-permute-start | bytes 2888 | tf_op jit(solution)/shard_map/ppermute | solution.py:20
  15.7 688.8 %reduce-scatter.4.cloned.1.call-start = ((), (), s32[]{:S(2)}) async-start(), calls=%async_computation.4 | async-start | bytes 983040
  273.7 2.5 copy-start.4
  273.7 2.5 copy-start.5
  273.7 2.5 copy-start.6
  273.7 2.5 copy-start.7
  551.6 28.5 %collective-permute-start.1 = (bf16[3,128]{1,0:T(4,128)(2,1)S(1)}, bf16[3,128]{1,0:T(4,128)(2,1)S(1)}, u32[]{:S(2)}, u32[]{:S(2)}) collective-permute-start(bf16[3,128]{1,0:T(4,128)(2,1)S(1)} %slice.323), channel_id=1, source_target_pairs={{0,4},{4,8},{8,12},{12,16},{16,20},{20,24},{24,28},{28,32},{32,36}... | collective-permute-start | bytes 2312 | tf_op jit(solution)/shard_map/ppermute | solution.py:20
  599.3 75.7 %collective-permute-start.2 = (bf16[15,384]{1,0:T(8,128)(2,1)S(1)}, bf16[15,384]{1,0:T(8,128)(2,1)S(1)}, u32[]{:S(2)}, u32[]{:S(2)}) collective-permute-start(bf16[15,384]{1,0:T(8,128)(2,1)S(1)} %get-tuple-element.44), channel_id=1, source_target_pairs={{0,4},{4,8},{8,12},{12,16},{16,20},{20,24},{24,28},{28,32},{32,36}... | collective-permute-start | bytes 34568 | tf_op jit(solution)/shard_map/ppermute | solution.py:30
  601.3 73.8 %collective-permute-start.3 = (bf16[15,384]{1,0:T(8,128)(2,1)S(1)}, bf16[15,384]{1,0:T(8,128)(2,1)S(1)}, u32[]{:S(2)}, u32[]{:S(2)}) collective-permute-start(bf16[15,384]{1,0:T(8,128)(2,1)S(1)} %get-tuple-element.45), channel_id=1, source_target_pairs={{4,0},{8,4},{12,8},{16,12},{20,16},{24,20},{28,24},{32,28},{36,32}... | collective-permute-start | bytes 34568 | tf_op jit(solution)/shard_map/ppermute | solution.py:31
  606.1 69.0 %copy-start.2 = (f32[384]{0:T(512)S(1)}, f32[384]{0:T(512)}, u32[]{:S(2)}) copy-start(f32[384]{0:T(512)} %param.18) | copy-start | bytes 4612
  606.1 69.0 %copy-start.3 = (f32[384]{0:T(512)S(1)}, f32[384]{0:T(512)}, u32[]{:S(2)}) copy-start(f32[384]{0:T(512)} %param.17) | copy-start | bytes 4612
Sparse Core Ops, SparseCore 0:
  9.5 225.2 all-gather.7
  237.0 216.6 all-gather.9
  455.8 216.8 all-gather.11
  678.2 26.1 reduce-scatter.3
where the time goes:
time: 714 us; the launch traced here: 713 us
  blocking collectives  540 us (76%)
  waiting for transfers between devices  121 us (17%)
  starting transfers between devices  14.8 us (2%)
  between operations  14.2 us (2%)
  local copies, waits for them, and re-layouts  10.8 us (2%)
    psum x1, blocking collectives, shards(): first_moment, squares = lax.psum((first_moment, squares), ('tm', 'mp'))  265 us
    all_gather x1, blocking collectives, shards(): lax.all_gather(sub_weight, ('dp', 'tm'), axis=0, tiled=True)  253 us
    all_gather x1, waiting for transfers between devices, shards(): shard_piece = lax.all_gather(out_weight, ('dp', 'tm'), axis=1, tiled=True)  66.6 us
    unnamed x5, waiting for transfers between devices  27.8 us
    ppermute x2, waiting for transfers between devices, shifted_2(): return lax.ppermute(block, axis, route)  26.3 us
  transfers between devices with their start and end apart: 8, of which 3 were waited for; matrix products, arithmetic and copies ran while one was open for 3% of the time, Pallas kernels for 0%

commit v1 on v0

v1 whole, which is shorter than its diff:
```python
import math

import jax
import jax.numpy as jnp
import numpy as np
from jax import lax
from jax.experimental import pallas as pl
from jax.experimental.pallas import tpu as pltpu
from jax.sharding import PartitionSpec as P

MEL = 128
WIN = 400
HOP = 160
STRIDE = 4
KERNEL = 31
BINS = 201
F32 = jnp.float32
BF16 = jnp.bfloat16
Z = 16
HOPS = (8, 7)
NT = (((1,), (1,)), ((), ()))


def mel_filters():
    mel_top = 2595.0 * math.log10(1.0 + 8000.0 / 700.0)
    borders = np.asarray(
        [
            700.0 * (10.0 ** (i * mel_top / (MEL + 1) / 2595.0) - 1.0) * WIN / 16000.0
            for i in range(MEL + 2)
        ],
        np.float32,
    )
    centers = np.arange(BINS, dtype=np.float32)[:, None]
    middle = borders[1:-1][None, :]
    lower = np.minimum(borders[:-2], borders[1:-1] - np.float32(1.0))[None, :]
    upper = np.maximum(borders[2:], borders[1:-1] + np.float32(1.0))[None, :]
    rising = (centers - lower) / (middle - lower)
    falling = (upper - centers) / (upper - middle)
    full = np.zeros((256, MEL), np.float32)
    full[:BINS] = np.maximum(np.float32(0.0), np.minimum(rising, falling))
    return full


def fourier_table():
    n = np.arange(WIN)
    window = 0.5 - 0.5 * np.cos(2.0 * np.pi * n / WIN)
    phases = 2.0 * np.pi * ((n[:, None] * np.arange(BINS)[None, :]) % WIN) / WIN
    full = np.zeros((512, 512), np.float32)
    full[:WIN, :BINS] = window[:, None] * np.cos(phases)
    full[:WIN, 256 : 256 + BINS] = window[:, None] * np.sin(phases)
    return full


def exact_dot(a, b):
    return jnp.dot(a, b, precision=lax.Precision.HIGHEST, preferred_element_type=F32)


def kernel(
    len_ref, wav, subw, valw, gatw, outw, dk, scale, shift, table, filters,
    out_ref,
    wbuf, halo, pack, packf, st1, compf, subr, vg, ow, subf, ma, mb, nm, fb, feats, normed,
    gp, gf, act, ps, rs,
    h_s, h_r, s1_s, s1_r, ma_s, ma_r, mb_s, mb_r, nm_s, nm_r, mh_s, mh_r, ag_s, ag_r,
    gh_s, gh_r, rs_s, rs_r, ring_s, ring_r, sib_s, sib_r,
):
    dp = lax.axis_index("dp")
    tm = lax.axis_index("tm")
    mp = lax.axis_index("mp")
    z_hi = tm // 8
    q = tm % 8
    core = tm % 2
    z = z_hi * 8 + dp
    length = len_ref[0]
    seg = tm * 4 + mp

    def remote(src, dst, ssem, rsem, **dev):
        return pltpu.make_async_remote_copy(
            src_ref=src, dst_ref=dst, send_sem=ssem, recv_sem=rsem,
            device_id=dev, device_id_type=pl.DeviceIdType.MESH,
        )

    tm_up, tm_down = (tm + 1) % 16, (tm + 15) % 16
    z_side = [(z + 1) % Z, (z + Z - 1) % Z]
    z_dev = [{"dp": s % 8, "tm": (s // 8) * 8 + q} for s in z_side]

    barrier = pltpu.get_barrier_semaphore()

    def greet(**dev):
        pl.semaphore_signal(
            barrier, inc=1, device_id=dev, device_id_type=pl.DeviceIdType.MESH
        )

    for i in range(1, 8):
        greet(tm=z_hi * 8 + (q + i) % 8)
    for dev in z_dev:
        greet(**dev)
    for i in range(4):
        if i:
            greet(mp=(mp + i) % 4)
        greet(tm=(1 - z_hi) * 8 + q, mp=(mp + i) % 4)
        greet(tm=tm_up, mp=(mp + i) % 4)
        greet(tm=tm_down, mp=(mp + i) % 4)

    packf[...] = jnp.zeros_like(packf)
    packf[0:7, :] = subw[...].astype(F32)
    packf[16:28, :] = valw[...].astype(F32)
    packf[32:44, :] = gatw[...].astype(F32)
    eye = (
        lax.broadcasted_iota(jnp.int32, (16, 12), 0)
        == lax.broadcasted_iota(jnp.int32, (16, 12), 1)
    ).astype(BF16)
    packf[48:64, :] = lax.dot_general(eye, outw[...], NT, preferred_element_type=F32)
    pack[...] = packf[...].astype(BF16)
    st1[q] = pack[...]

    pl.semaphore_wait(barrier, 7 + 2 + 3 + 4 + 8)

    prev_mp = (mp + 3) % 4
    prev_tm = (tm + 15 + (mp + 3) // 4) % 16
    halo_copy = remote(wav.at[0:8], halo, h_s, h_r, tm=prev_tm, mp=prev_mp)
    halo_copy.start()

    def stage1(i):
        return remote(
            pack, st1.at[q], s1_s.at[i], s1_r.at[i], tm=z_hi * 8 + (q + i) % 8
        )

    for i in range(1, 8):
        stage1(i).start()

    chains = {"S": (0, subr, 32), "V": (1, vg, 48), "O": (2, ow, 48)}

    def slot(chain, at, side):
        _, ref, rows = chains[chain]
        return ref.at[(at % 8) * 2 + at // 8, pl.ds(pl.multiple_of(side * rows, 16), rows)]

    def source(d, k):
        return (z + Z - k) % Z if d == 0 else (z + k) % Z

    def ring(chain, d, k):
        n = chains[chain][0]
        ref = slot(chain, source(d, k - 1), core)
        return remote(ref, ref, ring_s.at[n, d, k], ring_r.at[n, d, k], **z_dev[d])

    def ring_in(chain, d, k):
        n = chains[chain][0]
        ref = slot(chain, source(d, k), core)
        return remote(ref, ref, ring_s.at[n, d, k], ring_r.at[n, d, k], **z_dev[d])

    def sibling(chain, d, k, side):
        n = chains[chain][0]
        ref = slot(chain, source(d, k), side)
        return remote(
            ref, ref, sib_s.at[n, d, k], sib_r.at[n, d, k], tm=tm + 1 - 2 * core
        )

    def begin(chain):
        for d in range(2):
            ring(chain, d, 1).start()

    def serve(chain, first, last):
        for k in range(first, last + 1):
            for d in range(2):
                if k > HOPS[d]:
                    continue
                ring_in(chain, d, k).wait_recv()
                if k + 1 <= HOPS[d]:
                    ring(chain, d, k + 1).start()
                sibling(chain, d, k, core).start()

    def finish(chain):
        for d in range(2):
            for k in range(1, HOPS[d] + 1):
                sibling(chain, d, k, 1 - core).wait_recv()

    def drain(chain):
        for d in range(2):
            for k in range(1, HOPS[d] + 1):
                ring(chain, d, k).wait_send()
                sibling(chain, d, k, core).wait_send()

    position = (
        seg * 40960
        + lax.broadcasted_iota(jnp.int32, (328, 128), 0) * 128
        + lax.broadcasted_iota(jnp.int32, (328, 128), 1)
    )
    wbuf[0:320] = jnp.where(position[:320] < length, wav[...], 0.0)

    for i in range(1, 8):
        stage1(i).wait_recv()
    for i in range(8):
        block = st1[i].astype(F32)
        compf[7 * i : 7 * i + 7, 0:384] = block[0:7]
        for j in range(3):
            compf[64 + 12 * i : 76 + 12 * i, 384 * j : 384 * j + 384] = block[
                16 * j + 16 : 16 * j + 28
            ]
    compf[56:64, 0:384] = jnp.zeros((8, 384), F32)
    mine = (z % 8) * 2 + z // 8
    subr[mine] = compf[0:64, 0:384].astype(BF16)
    vg[mine] = compf[64:160, 0:768].astype(BF16)
    ow[mine] = compf[64:160, 768:1152].astype(BF16)
    begin("S")
    begin("V")

    halo_copy.wait_recv()
    wbuf[320:328] = jnp.where(position[320:328] < length, halo[...], 0.0)
    wide = jnp.concatenate([wbuf[pl.ds(c, 64, stride=5), :] for c in range(7)], axis=1)
    frames = jnp.concatenate(
        [wide[:, :512]]
        + [pltpu.roll(wide, 896 - HOP * j, 1)[:, :512] for j in range(1, STRIDE)],
        axis=0,
    )
    spectrum = exact_dot(frames, table[...])
    power = spectrum[:, :256] * spectrum[:, :256] + spectrum[:, 256:] * spectrum[:, 256:]
    log_energy = jnp.log(exact_dot(power, filters[...]) + 1e-06)
    row = lax.broadcasted_iota(jnp.int32, (256, MEL), 0)
    valid_mel = seg * 256 + (row % 64) * 4 + row // 64 < length // HOP
    kept = jnp.where(valid_mel, log_energy, 0.0)
    ma[q] = jnp.concatenate(
        [
            jnp.sum(kept, axis=0, keepdims=True),
            jnp.sum(kept * kept, axis=0, keepdims=True),
            jnp.zeros((6, MEL), F32),
        ],
        axis=0,
    )

    def moments_a(i):
        return remote(
            ma.at[q], ma.at[q], ma_s.at[i], ma_r.at[i], tm=z_hi * 8 + (q + i) % 8
        )

    for i in range(1, 8):
        moments_a(i).start()
    serve("S", 1, 2)
    for i in range(1, 8):
        moments_a(i).wait_recv()
    total = ma[0]
    for i in range(1, 8):
        total = total + ma[i]
    place = z_hi * 4 + mp
    mb[place] = total

    def moments_b(i):
        other = (place + i) % 8
        return remote(
            mb.at[place], mb.at[place], mb_s.at[i], mb_r.at[i],
            tm=(other // 4) * 8 + q, mp=other % 4,
        )

    for i in range(1, 8):
        moments_b(i).start()
    serve("S", 3, 4)
    serve("V", 1, 1)
    for i in range(1, 8):
        moments_b(i).wait_recv()
    total = mb[0]
    for i in range(1, 8):
        total = total + mb[i]
    count = (length // HOP).astype(F32)
    mel_mean = total[0:1] / count
    mel_var = total[1:2] / count - mel_mean * mel_mean
    normed_mel = jnp.where(
        valid_mel, (log_energy - mel_mean) * lax.rsqrt(mel_var + 1e-05), 0.0
    ).astype(BF16)
    own = pl.ds(pl.multiple_of(16 + mp * 64, 16), 64)
    for j in range(STRIDE):
        nm[j, own, :] = normed_mel[j * 64 : j * 64 + 64]

    def mel_gather(i):
        ref = nm.at[:, own, :]
        return remote(ref, ref, nm_s.at[i], nm_r.at[i], mp=(mp + i) % 4)

    def mel_gather_in(i):
        there = pl.ds(pl.multiple_of(16 + ((mp + 4 - i) % 4) * 64, 16), 64)
        ref = nm.at[:, there, :]
        return remote(ref, ref, nm_s.at[i], nm_r.at[i], mp=(mp + i) % 4)

    def mel_halo(i):
        return remote(
            nm.at[:, pl.ds(256, 16), :], nm.at[:, pl.ds(0, 16), :],
            mh_s.at[i], mh_r, tm=tm_up, mp=(mp + i) % 4,
        )

    for i in range(1, 4):
        mel_gather(i).start()

    @pl.when(mp == 3)
    def _():
        for i in range(4):
            mel_halo(i).start()

    serve("S", 5, 6)
    serve("V", 2, 2)
    serve("S", 7, 8)
    serve("V", 3, 3)
    begin("O")
    finish("S")
    for s in range(Z):
        subf[56 * s : 56 * s + 56, :] = subr[s].astype(F32)[0:56]
    for i in range(1, 4):
        mel_gather_in(i).wait_recv()
    mel_halo(0).wait_recv()

    head = subf[0:384, :].astype(BF16)
    rest = subf[384:896, :].astype(BF16)
    before = jnp.dot(
        jnp.concatenate([nm[j] for j in range(1, STRIDE)], axis=1), head,
        preferred_element_type=F32,
    )
    edge = lax.broadcasted_iota(jnp.int32, (272, 384), 0) < jnp.where(tm == 0, 16, 0)
    fb[...] = jnp.where(edge, 0.0, before)
    here = jnp.dot(
        jnp.concatenate([nm[j, 16:272] for j in range(STRIDE)], axis=1), rest,
        preferred_element_type=F32,
    )
    feats[mp] = (here + fb[15:271, :]).astype(BF16)

    def gather(i):
        return remote(
            feats.at[mp], feats.at[mp], ag_s.at[i], ag_r.at[i], mp=(mp + i) % 4
        )

    def gather_in(i):
        ref = feats.at[(mp + 4 - i) % 4]
        return remote(ref, ref, ag_s.at[i], ag_r.at[i], mp=(mp + i) % 4)

    for i in range(1, 4):
        gather(i).start()
    serve("V", 4, 5)
    serve("O", 1, 1)
    serve("V", 6, 7)
    serve("O", 2, 2)
    serve("V", 8, 8)
    serve("O", 3, 4)
    for i in range(1, 4):
        gather_in(i).wait_recv()

    @pl.loop(0, 8)
    def _(b):
        rows = pl.ds(pl.multiple_of(b * 32, 32), 32)
        wide = jnp.concatenate([feats[g, rows, :] for g in range(4)], axis=1).astype(F32)
        centered = wide - jnp.mean(wide, axis=1, keepdims=True)
        spread = jnp.mean(centered * centered, axis=1, keepdims=True)
        normed[rows, :] = (centered * lax.rsqrt(spread + 1e-05)).astype(BF16)

    finish("V")
    both = jnp.dot(
        normed[...], vg[...].reshape(1536, 768), preferred_element_type=F32
    )
    valid = (
        tm * 256 + lax.broadcasted_iota(jnp.int32, (256, 384), 0)
        < length // (STRIDE * HOP)
    )
    gated = jnp.where(valid, both[:, :384] * jax.nn.sigmoid(both[:, 384:]), 0.0)
    gp[16:272, :] = gated.astype(BF16)

    to_next = remote(
        gp.at[pl.ds(256, 16)], gp.at[pl.ds(0, 16)], gh_s.at[0], gh_r.at[0], tm=tm_up
    )
    to_prev = remote(
        gp.at[pl.ds(16, 16)], gp.at[pl.ds(272, 16)], gh_s.at[1], gh_r.at[1], tm=tm_down
    )
    to_next.start()
    to_prev.start()
    serve("O", 5, 6)
    gf[16:272, :] = gp[16:272, :].astype(F32)
    to_next.wait_recv()
    to_prev.wait_recv()
    gf[0:16, :] = jnp.where(tm == 0, 0.0, gp[0:16, :].astype(F32))
    gf[272:288, :] = jnp.where(tm == 15, 0.0, gp[272:288, :].astype(F32))

    @pl.loop(0, 12)
    def _(b):
        rows = pl.multiple_of((b // 3) * 64, 64)
        lanes = pl.ds(pl.multiple_of((b % 3) * 128, 128), 128)
        window = gf[pl.ds(rows, 96), lanes]
        taps = dk[:, lanes]
        out = jnp.zeros((64, 128), F32)
        for p in range(8):
            part = jnp.zeros((72, 128), F32)
            for w in range(4):
                tap = 8 * w + p - 1
                if tap >= 0:
                    part = part + taps[tap : tap + 1] * window[8 * w : 8 * w + 72]
            if p:
                part = pltpu.roll(part, 72 - p, 0)
            out = out + part[:64]
        moved = out * scale[:, lanes] + shift[:, lanes]
        act[pl.ds(rows, 64), lanes] = (moved * jax.nn.sigmoid(moved)).astype(BF16)

    serve("O", 7, 8)
    finish("O")

    def partial(g):
        block = ow[pl.ds(g * 4, 4)].reshape(384, 384)
        return lax.dot_general(
            act[...], block, NT, preferred_element_type=F32
        ).astype(BF16)

    def scatter(i):
        return remote(ps.at[i], rs.at[i], rs_s.at[i], rs_r.at[i], mp=(mp + i) % 4)

    for i in (2, 1, 3):
        ps[i] = partial((mp + i) % 4)
        scatter(i).start()
    summed = partial(mp).astype(F32)
    for i in range(1, 4):
        scatter(i).wait_recv()
        summed = summed + rs[i].astype(F32)
    out_ref[...] = jnp.where(valid, feats[mp].astype(F32) + summed, 0.0).astype(BF16)

    halo_copy.wait_send()
    for i in range(1, 8):
        stage1(i).wait_send()
        moments_a(i).wait_send()
        moments_b(i).wait_send()
    for i in range(1, 4):
        mel_gather(i).wait_send()
        gather(i).wait_send()
        scatter(i).wait_send()

    @pl.when(mp == 3)
    def _():
        for i in range(4):
            mel_halo(i).wait_send()

    to_next.wait_send()
    to_prev.wait_send()
    for chain in "SVO":
        drain(chain)


def shards(
    waveform, lengths, sub_weight, value_weight, gate_weight, out_weight,
    depth_kernel, norm_scale, norm_shift,
):
    vmem = pl.BlockSpec(memory_space=pltpu.VMEM)
    dma = pltpu.SemaphoreType.DMA
    encoded = pl.pallas_call(
        kernel,
        out_shape=jax.ShapeDtypeStruct((256, 384), BF16),
        in_specs=[pl.BlockSpec(memory_space=pltpu.SMEM)] + [vmem] * 10,
        out_specs=vmem,
        scratch_shapes=[
            pltpu.VMEM((328, 128), F32),
            pltpu.VMEM((8, 128), F32),
            pltpu.VMEM((64, 384), BF16),
            pltpu.VMEM((64, 384), F32),
            pltpu.VMEM((8, 64, 384), BF16),
            pltpu.VMEM((160, 1152), F32),
            pltpu.VMEM((Z, 64, 384), BF16),
            pltpu.VMEM((Z, 96, 768), BF16),
            pltpu.VMEM((Z, 96, 384), BF16),
            pltpu.VMEM((896, 384), F32),
            pltpu.VMEM((8, 8, 128), F32),
            pltpu.VMEM((8, 8, 128), F32),
            pltpu.VMEM((4, 272, 128), BF16),
            pltpu.VMEM((272, 384), F32),
            pltpu.VMEM((4, 256, 384), BF16),
            pltpu.VMEM((256, 1536), BF16),
            pltpu.VMEM((288, 384), BF16),
            pltpu.VMEM((288, 384), F32),
            pltpu.VMEM((256, 384), BF16),
            pltpu.VMEM((4, 256, 384), BF16),
            pltpu.VMEM((4, 256, 384), BF16),
            dma, dma,
            dma((8,)), dma((8,)),
            dma((8,)), dma((8,)),
            dma((8,)), dma((8,)),
            dma((4,)), dma((4,)),
            dma((4,)), dma,
            dma((4,)), dma((4,)),
            dma((2,)), dma((2,)),
            dma((4,)), dma((4,)),
            dma((3, 2, 9)), dma((3, 2, 9)),
            dma((3, 2, 9)), dma((3, 2, 9)),
        ],
        compiler_params=pltpu.CompilerParams(
            collective_id=0, has_side_effects=True, vmem_limit_bytes=48 * 1024 * 1024
        ),
    )(
        lengths,
        waveform.reshape(320, 128),
        sub_weight,
        value_weight,
        gate_weight,
        out_weight,
        depth_kernel,
        norm_scale.reshape(1, 384),
        norm_shift.reshape(1, 384),
        jnp.asarray(fourier_table()),
        jnp.asarray(mel_filters()),
    )
    return encoded[None]


def solution(mesh):
    placed = (
        P("dp", ("tm", "mp")),
        P("dp"),
        P(("dp", "tm"), "mp"),
        P(("dp", "tm"), "mp"),
        P(("dp", "tm"), "mp"),
        P("mp", ("dp", "tm")),
        P(None, "mp"),
        P("mp"),
        P("mp"),
    )
    return jax.shard_map(
        shards, mesh=mesh, in_specs=placed, out_specs=P("dp", "tm", "mp"), check_vma=False
    )
```

time: 714 us -> 107 us (0.15)
  blocking collectives: 540 us -> 0 us
  waiting for transfers between devices: 121 us -> 0 us
  Pallas kernels: 0 us -> 100 us
  starting transfers between devices: 14.8 us -> 0 us
  between operations: 14.2 us -> 0.75 us
    all_gather x3 -> x0, blocking collectives: 275 us -> none  [the longest x1 253 us: shards(): lax.all_gather(sub_weight, ('dp', 'tm'), axis=0, tiled=True)]
    psum x1 -> x0, blocking collectives: 265 us -> none  [shards(): first_moment, squares = lax.psum((first_moment, squares), ('tm', 'mp'))]
    pallas_call x0 -> x1, Pallas kernels: none -> 100 us  [shards(): pl.pallas_call(kernel, out_shape=jax.ShapeDtypeStruct((256, 384), BF16),...]
    all_gather x3 -> x0, waiting for transfers between devices: 66.7 us -> none  [the longest x1 66.6 us: shards(): shard_piece = lax.all_gather(out_weight, ('dp', 'tm'), axis=1, tiled=True)]
    unnamed x5 -> x0, waiting for transfers between devices: 27.8 us -> none
    ppermute x4 -> x0, waiting for transfers between devices: 26.3 us -> none  [the longest x2 26.3 us: shifted_2(): return lax.ppermute(block, axis, route)]
    ppermute x4 -> x0, starting transfers between devices: 14.7 us -> none  [the longest x2 7.94 us: shifted_2(): return lax.ppermute(block, axis, route)]
  transfers between devices with their start and end apart: 8 -> 0, of which waited for: 3 -> 0; matrix products, arithmetic and copies ran while one was open for 3% -> 0% of each run, Pallas kernels for 0% -> 0%
where the time goes in v1:
time: 107 us; the launch traced here: 106 us
  Pallas kernels  100 us (93%)
  local copies, waits for them, and re-layouts  5.32 us (5%)
    pallas_call x1, Pallas kernels, shards(): pl.pallas_call(kernel, out_shape=jax.ShapeDtypeStruct((256, 384), BF16),...  100 us
    unnamed x20, local copies, waits for them, and re-layouts  5.31 us

profile of v1, /device:TPU:1, one launch (start us, length us, event | category | flops | bytes accessed | tf_op | source)
XLA Modules:
  0.0 106.4 jit_solution(11428028991193518010)
XLA Ops:
  0.0 0.0 copy-start.7
  0.7 0.0 copy-done.7
  0.7 0.0 copy-start.8
  0.7 0.7 copy-done.8
  1.4 0.0 copy-start.3
  1.4 0.0 copy-start.4
  1.4 0.0 copy-start.5
  1.4 0.0 copy-start.6
  1.4 0.9 copy.12.outw
  2.3 0.0 copy-done.3
  2.3 0.0 copy-done.4
  2.3 0.0 copy-done.5
  2.3 0.0 copy-done.6
  2.3 0.0 copy-start
  2.3 1.2 %copy-done = f32[512,512]{1,0:T(8,128)S(1)} copy-done((f32[512,512]{1,0:T(8,128)S(1)}, f32[512,512]{1,0:T(8,128)}, u32[]{:S(2)}) %copy-start) | copy-done | bytes 1048600
  3.6 0.0 copy-start.1
  3.6 0.9 copy-done.1
  4.5 0.0 copy-start.2
  4.5 0.9 copy-done.2
  5.4 100.4 %shard_map.109 = bf16[256,384]{1,0:T(8,128)(2,1)S(1)} custom-call(s32[1]{0:T(128)S(6)} %copy.14.len_ref, f32[320,128]{1,0:T(8,128)S(1)} %bitcast.3, bf16[7,384]{1,0:T(8,128)(2,1)S(1)} %copy-done.6, bf16[12,384]{1,0:T(8,128)(2,1)S(1)} %copy-done.4, bf16[12,384]{1,0:T(8,128)(2,1)S(1)} %copy-done.5, bf16[384,12]{1,0:T(8,128)(2,1)S(1)} %copy.12.outw, ...), custom_call_target="tpu_custom_call" | custom-call | tf_op jit(solution)/shard_map/pallas_call | solution.py:441
  105.8 0.7 copy.15
  (2 shorter events, 0.0 us)
Async XLA Ops:
  0.0 0.7 copy-start.7
  0.7 0.7 copy-start.8
  1.4 0.9 copy-start.3
  1.4 0.9 copy-start.4
  1.4 0.9 copy-start.5
  1.4 0.9 copy-start.6
  2.3 1.2 %copy-start = (f32[512,512]{1,0:T(8,128)S(1)}, f32[512,512]{1,0:T(8,128)}, u32[]{:S(2)}) copy-start(f32[512,512]{1,0:T(8,128)} %constant.4.clone.table) | copy-start | bytes 3145732
  3.6 0.9 copy-start.1
  4.5 0.9 copy-start.2

commit v2 on v1

v2 whole, which is shorter than its diff:
```python
import math

import jax
import jax.numpy as jnp
import numpy as np
from jax import lax
from jax.experimental import pallas as pl
from jax.experimental.pallas import tpu as pltpu
from jax.sharding import PartitionSpec as P

MEL = 128
WIN = 400
HOP = 160
STRIDE = 4
KERNEL = 31
BINS = 201
F32 = jnp.float32
BF16 = jnp.bfloat16
Z = 16
NT = (((1,), (1,)), ((), ()))


def mel_filters():
    mel_top = 2595.0 * math.log10(1.0 + 8000.0 / 700.0)
    borders = np.asarray(
        [
            700.0 * (10.0 ** (i * mel_top / (MEL + 1) / 2595.0) - 1.0) * WIN / 16000.0
            for i in range(MEL + 2)
        ],
        np.float32,
    )
    centers = np.arange(BINS, dtype=np.float32)[:, None]
    middle = borders[1:-1][None, :]
    lower = np.minimum(borders[:-2], borders[1:-1] - np.float32(1.0))[None, :]
    upper = np.maximum(borders[2:], borders[1:-1] + np.float32(1.0))[None, :]
    rising = (centers - lower) / (middle - lower)
    falling = (upper - centers) / (upper - middle)
    full = np.zeros((256, MEL), np.float32)
    full[:BINS] = np.maximum(np.float32(0.0), np.minimum(rising, falling))
    return full


def fourier_table():
    n = np.arange(WIN)
    window = 0.5 - 0.5 * np.cos(2.0 * np.pi * n / WIN)
    phases = 2.0 * np.pi * ((n[:, None] * np.arange(BINS)[None, :]) % WIN) / WIN
    full = np.zeros((512, 512), np.float32)
    full[:WIN, :BINS] = window[:, None] * np.cos(phases)
    full[:WIN, 256 : 256 + BINS] = window[:, None] * np.sin(phases)
    return full


def exact_dot(a, b):
    return jnp.dot(a, b, precision=lax.Precision.HIGHEST, preferred_element_type=F32)


def kernel(
    len_ref, subw, valw, gatw, outw, wav_hbm, dk_hbm, scale, shift, table_hbm, filters_hbm,
    out_ref,
    wav, dk, table, filters, wbuf, halo, pack, packf, got, own48, w, sf, vw, gw, ow,
    ma, mb, le, nmf, feats, normed, gp, gf, act, ps, rs,
    in_s, h_s, h_r, c_s, c_r, ma_s, ma_r, mb_s, mb_r, le_s, le_r, lh_s, lh_r, ag_s, ag_r,
    gh_s, gh_r, rs_s, rs_r, z_s, z_r, x_s, x_r, sib_s, sib_r,
):
    dp = lax.axis_index("dp")
    tm = lax.axis_index("tm")
    mp = lax.axis_index("mp")
    z_hi = tm // 8
    q = tm % 8
    x = q // 2
    core = tm % 2
    z = z_hi * 8 + dp
    slab = dp * 2 + z_hi
    length = len_ref[0]
    seg = tm * 4 + mp
    tm_up, tm_down = (tm + 1) % 16, (tm + 15) % 16
    twin = tm + 1 - 2 * core

    def remote(src, dst, ssem, rsem, **dev):
        return pltpu.make_async_remote_copy(
            src_ref=src, dst_ref=dst, send_sem=ssem, recv_sem=rsem,
            device_id=dev, device_id_type=pl.DeviceIdType.MESH,
        )

    loads = [
        pltpu.make_async_copy(there, here, in_s.at[i])
        for i, (there, here) in enumerate(
            [(wav_hbm, wav), (table_hbm, table), (filters_hbm, filters), (dk_hbm, dk)]
        )
    ]
    for load in loads:
        load.start()

    barrier = pltpu.get_barrier_semaphore()

    def greet(**dev):
        pl.semaphore_signal(
            barrier, inc=1, device_id=dev, device_id_type=pl.DeviceIdType.MESH
        )

    def along_z(i):
        other = (z + i) % Z
        return {"dp": other % 8, "tm": (other // 8) * 8 + q}

    for i in range(1, Z):
        greet(**along_z(i))
    for i in range(1, 8):
        greet(tm=z_hi * 8 + (q + i) % 8)
    for i in range(4):
        if i:
            greet(mp=(mp + i) % 4)
            greet(tm=(1 - z_hi) * 8 + q, mp=(mp + i) % 4)
        greet(tm=tm_up, mp=(mp + i) % 4)
        greet(tm=tm_down, mp=(mp + i) % 4)

    packf[...] = jnp.zeros_like(packf)
    packf[0, 0:7, :] = subw[...].astype(F32)
    packf[0, 7:19, :] = outw[...].astype(F32)
    packf[1, 0:12, :] = valw[...].astype(F32)
    packf[1, 12:24, :] = gatw[...].astype(F32)
    pack[...] = packf[...].astype(BF16)

    pl.semaphore_wait(barrier, 15 + 7 + 3 + 3 + 8)

    swap = remote(pack.at[1 - core], got, c_s, c_r, tm=twin)
    swap.start()
    loads[0].wait()
    prev_mp = (mp + 3) % 4
    prev_tm = (tm + 15 + (mp + 3) // 4) % 16
    halo_copy = remote(wav.at[0:8], halo, h_s, h_r, tm=prev_tm, mp=prev_mp)
    halo_copy.start()

    position = (
        seg * 40960
        + lax.broadcasted_iota(jnp.int32, (328, 128), 0) * 128
        + lax.broadcasted_iota(jnp.int32, (328, 128), 1)
    )
    wbuf[0:320] = jnp.where(position[:320] < length, wav[...], 0.0)

    swap.wait_recv()
    mine, other = packf[core], got[...].astype(F32)
    first = jnp.where(core == 0, mine, other)
    second = jnp.where(core == 0, other, mine)

    @pl.when(core == 0)
    def _():
        own48[0:7] = first[0:7]
        own48[7:14] = second[0:7]
        own48[14:16] = jnp.zeros((2, 384), F32)
        own48[16:28] = first[7:19]
        own48[28:40] = second[7:19]
        own48[40:48] = jnp.zeros((8, 384), F32)

    @pl.when(core == 1)
    def _():
        own48[0:12] = first[0:12]
        own48[12:24] = second[0:12]
        own48[24:36] = first[12:24]
        own48[36:48] = second[12:24]

    batch = [core * 3 + j for j in range(3)]
    for j in range(3):
        w[batch[j], slab, x] = own48[16 * j : 16 * j + 16].astype(BF16)

    def push_z(j, i):
        ref = w.at[batch[j], slab, x]
        return remote(ref, ref, z_s.at[j, i], z_r.at[j, i], **along_z(i))

    def from_z(j, i):
        at = (z + Z - i) % Z
        ref = w.at[batch[j], (at % 8) * 2 + at // 8, x]
        return remote(ref, ref, z_s.at[j, i], z_r.at[j, i], **along_z(i))

    def push_x(j, i):
        ref = w.at[batch[j], :, x]
        return remote(
            ref, ref, x_s.at[j, i], x_r.at[j, i],
            tm=z_hi * 8 + ((x + i) % 4) * 2 + core,
        )

    def from_x(j, i):
        ref = w.at[batch[j], :, (x + 4 - i) % 4]
        return remote(
            ref, ref, x_s.at[j, i], x_r.at[j, i],
            tm=z_hi * 8 + ((x + i) % 4) * 2 + core,
        )

    def push_twin(j):
        ref = w.at[batch[j]]
        return remote(ref, ref, sib_s.at[j], sib_r.at[j], tm=twin)

    def from_twin(j):
        ref = w.at[(1 - core) * 3 + j]
        return remote(ref, ref, sib_s.at[j], sib_r.at[j], tm=twin)

    def send_z(j):
        for i in (8, 7, 9, 6, 10, 5, 11, 4, 12, 3, 13, 2, 14, 1, 15):
            push_z(j, i).start()

    def send_x(j):
        for i in range(1, Z):
            from_z(j, i).wait_recv()
        for i in (2, 1, 3):
            push_x(j, i).start()

    def send_twin(j):
        for i in range(1, 4):
            from_x(j, i).wait_recv()
        push_twin(j).start()

    send_z(0)

    halo_copy.wait_recv()
    wbuf[320:328] = jnp.where(position[320:328] < length, halo[...], 0.0)
    wide = jnp.concatenate([wbuf[pl.ds(c, 64, stride=5), :] for c in range(7)], axis=1)
    frames = jnp.concatenate(
        [wide[:, :512]]
        + [pltpu.roll(wide, 896 - HOP * j, 1)[:, :512] for j in range(1, STRIDE)],
        axis=0,
    )
    loads[1].wait()
    loads[2].wait()
    spectrum = exact_dot(frames, table[...])
    power = spectrum[:, :256] * spectrum[:, :256] + spectrum[:, 256:] * spectrum[:, 256:]
    log_energy = jnp.log(exact_dot(power, filters[...]) + 1e-06)
    row = lax.broadcasted_iota(jnp.int32, (256, MEL), 0)
    valid_mel = seg * 256 + (row % 64) * 4 + row // 64 < length // HOP
    kept = jnp.where(valid_mel, log_energy, 0.0)
    ma[q] = jnp.concatenate(
        [
            jnp.sum(kept, axis=0, keepdims=True),
            jnp.sum(kept * kept, axis=0, keepdims=True),
            jnp.zeros((6, MEL), F32),
        ],
        axis=0,
    )

    def moments_a(i):
        return remote(
            ma.at[q], ma.at[q], ma_s.at[i], ma_r.at[i], tm=z_hi * 8 + (q + i) % 8
        )

    for i in range(1, 8):
        moments_a(i).start()

    own = pl.ds(pl.multiple_of(8 + mp * 64, 8), 64)
    for j in range(STRIDE):
        le[j, own, :] = log_energy[j * 64 : j * 64 + 64]

    def mel_gather(i):
        ref = le.at[:, own, :]
        return remote(ref, ref, le_s.at[i], le_r.at[i], mp=(mp + i) % 4)

    def mel_gather_in(i):
        there = pl.ds(pl.multiple_of(8 + ((mp + 4 - i) % 4) * 64, 8), 64)
        ref = le.at[:, there, :]
        return remote(ref, ref, le_s.at[i], le_r.at[i], mp=(mp + i) % 4)

    def mel_halo(i):
        return remote(
            le.at[:, pl.ds(256, 8), :], le.at[:, pl.ds(0, 8), :],
            lh_s.at[i], lh_r, tm=tm_up, mp=(mp + i) % 4,
        )

    @pl.when(mp == 3)
    def _():
        for i in range(4):
            mel_halo(i).start()

    for i in (2, 1, 3):
        mel_gather(i).start()
    for i in range(1, 8):
        moments_a(i).wait_recv()
    total = ma[0]
    for i in range(1, 8):
        total = total + ma[i]
    place = z_hi * 4 + mp
    mb[place] = total

    def moments_b(i):
        away = (place + i) % 8
        return remote(
            mb.at[place], mb.at[place], mb_s.at[i], mb_r.at[i],
            tm=(away // 4) * 8 + q, mp=away % 4,
        )

    for i in (4, 5, 6, 7, 3, 2, 1):
        moments_b(i).start()
    send_z(1)
    send_x(0)
    send_z(2)
    for i in range(1, 8):
        moments_b(i).wait_recv()
    total = mb[0]
    for i in range(1, 8):
        total = total + mb[i]
    count = (length // HOP).astype(F32)
    mel_mean = total[0:1] / count
    mel_var = total[1:2] / count - mel_mean * mel_mean
    mel_scale = lax.rsqrt(mel_var + 1e-05)
    for i in range(1, 4):
        mel_gather_in(i).wait_recv()
    mel_halo(0).wait_recv()
    time = tm * 256 - 8 + lax.broadcasted_iota(jnp.int32, (264, MEL), 0)
    for j in range(STRIDE):
        known = (time >= 0) & (time * 4 + j < length // HOP)
        nmf[j] = jnp.where(known, (le[j] - mel_mean) * mel_scale, 0.0)

    send_x(1)
    send_twin(0)
    from_twin(0).wait_recv()

    for s in range(Z):
        for i in range(4):
            sf[56 * s + 14 * i : 56 * s + 14 * i + 14, :] = w[0, s, i].astype(F32)[0:14]
    stacked = jnp.concatenate(
        [nmf[j, 7:263] for j in range(1, STRIDE)] + [nmf[j, 8:264] for j in range(STRIDE)],
        axis=1,
    ).astype(BF16)
    feats[mp] = jnp.dot(
        stacked, sf[...].astype(BF16), preferred_element_type=F32
    ).astype(BF16)

    def gather(i):
        return remote(
            feats.at[mp], feats.at[mp], ag_s.at[i], ag_r.at[i], mp=(mp + i) % 4
        )

    def gather_in(i):
        ref = feats.at[(mp + 4 - i) % 4]
        return remote(ref, ref, ag_s.at[i], ag_r.at[i], mp=(mp + i) % 4)

    for i in (2, 1, 3):
        gather(i).start()
    send_x(2)
    send_twin(1)
    send_twin(2)

    for i in range(1, 4):
        gather_in(i).wait_recv()

    @pl.loop(0, 8)
    def _(b):
        rows = pl.ds(pl.multiple_of(b * 32, 32), 32)
        wide = jnp.concatenate([feats[g, rows, :] for g in range(4)], axis=1).astype(F32)
        centered = wide - jnp.mean(wide, axis=1, keepdims=True)
        spread = jnp.mean(centered * centered, axis=1, keepdims=True)
        normed[rows, :] = (centered * lax.rsqrt(spread + 1e-05)).astype(BF16)

    from_twin(1).wait_recv()
    from_twin(2).wait_recv()

    @pl.loop(0, Z)
    def _(s):
        value, gate = [], []
        for i in range(4):
            top, middle, bottom = (w[b, s, i].astype(F32) for b in (3, 4, 5))
            value += [top, middle[0:8]]
            gate += [middle[8:16], bottom]
        vw[s] = jnp.concatenate(value, axis=0).astype(BF16)
        gw[s] = jnp.concatenate(gate, axis=0).astype(BF16)

    value_sum = jnp.dot(
        normed[...], vw[...].reshape(1536, 384), preferred_element_type=F32
    )
    gate_sum = jnp.dot(
        normed[...], gw[...].reshape(1536, 384), preferred_element_type=F32
    )
    valid = (
        tm * 256 + lax.broadcasted_iota(jnp.int32, (256, 384), 0)
        < length // (STRIDE * HOP)
    )
    gated = jnp.where(valid, value_sum * jax.nn.sigmoid(gate_sum), 0.0)
    gp[16:272, :] = gated.astype(BF16)

    to_next = remote(
        gp.at[pl.ds(256, 16)], gp.at[pl.ds(0, 16)], gh_s.at[0], gh_r.at[0], tm=tm_up
    )
    to_prev = remote(
        gp.at[pl.ds(16, 16)], gp.at[pl.ds(272, 16)], gh_s.at[1], gh_r.at[1], tm=tm_down
    )
    to_next.start()
    to_prev.start()
    gf[16:272, :] = gp[16:272, :].astype(F32)
    loads[3].wait()

    def depthwise(block, column):
        rows = pl.multiple_of(block * 64, 64)
        lanes = pl.ds(pl.multiple_of(column * 128, 128), 128)
        window = gf[pl.ds(rows, 96), lanes]
        taps = dk[:, lanes]
        out = jnp.zeros((64, 128), F32)
        for p in range(8):
            part = jnp.zeros((72, 128), F32)
            for k in range(4):
                tap = 8 * k + p - 1
                if tap >= 0:
                    part = part + taps[tap : tap + 1] * window[8 * k : 8 * k + 72]
            if p:
                part = pltpu.roll(part, 72 - p, 0)
            out = out + part[:64]
        moved = out * scale[lanes].reshape(1, 128) + shift[lanes].reshape(1, 128)
        act[pl.ds(rows, 64), lanes] = (moved * jax.nn.sigmoid(moved)).astype(BF16)

    @pl.loop(0, 6)
    def _(b):
        depthwise(b // 3 + 1, b % 3)

    to_next.wait_recv()
    to_prev.wait_recv()
    gf[0:16, :] = jnp.where(tm == 0, 0.0, gp[0:16, :].astype(F32))
    gf[272:288, :] = jnp.where(tm == 15, 0.0, gp[272:288, :].astype(F32))

    @pl.loop(0, 6)
    def _(b):
        depthwise((b // 3) * 3, b % 3)

    @pl.loop(0, Z)
    def _(s):
        rows = []
        for i in range(4):
            rows += [w[1, s, i].astype(F32), w[2, s, i].astype(F32)[0:8]]
        ow[s] = jnp.concatenate(rows, axis=0).astype(BF16)

    def partial(g):
        block = ow[pl.ds(g * 4, 4)].reshape(384, 384)
        return lax.dot_general(
            act[...], block, NT, preferred_element_type=F32
        ).astype(BF16)

    def scatter(i):
        return remote(ps.at[i], rs.at[i], rs_s.at[i], rs_r.at[i], mp=(mp + i) % 4)

    for i in (2, 1, 3):
        ps[i] = partial((mp + i) % 4)
        scatter(i).start()
    summed = partial(mp).astype(F32)
    for i in range(1, 4):
        scatter(i).wait_recv()
        summed = summed + rs[i].astype(F32)
    out_ref[...] = jnp.where(valid, feats[mp].astype(F32) + summed, 0.0).astype(BF16)

    halo_copy.wait_send()
    swap.wait_send()
    for i in range(1, 8):
        moments_a(i).wait_send()
        moments_b(i).wait_send()
    for i in range(1, 4):
        mel_gather(i).wait_send()
        gather(i).wait_send()
        scatter(i).wait_send()

    @pl.when(mp == 3)
    def _():
        for i in range(4):
            mel_halo(i).wait_send()

    to_next.wait_send()
    to_prev.wait_send()
    for j in range(3):
        for i in range(1, Z):
            push_z(j, i).wait_send()
        for i in range(1, 4):
            push_x(j, i).wait_send()
        push_twin(j).wait_send()


def shards(
    waveform, lengths, sub_weight, value_weight, gate_weight, out_weight,
    depth_kernel, norm_scale, norm_shift,
):
    vmem = pl.BlockSpec(memory_space=pltpu.VMEM)
    hbm = pl.BlockSpec(memory_space=pltpu.HBM)
    dma = pltpu.SemaphoreType.DMA
    encoded = pl.pallas_call(
        kernel,
        out_shape=jax.ShapeDtypeStruct((256, 384), BF16),
        in_specs=[pl.BlockSpec(memory_space=pltpu.SMEM)] + [vmem] * 4 + [hbm] * 2 + [vmem] * 2 + [hbm] * 2,
        out_specs=vmem,
        scratch_shapes=[
            pltpu.VMEM((320, 128), F32),
            pltpu.VMEM((KERNEL, 384), F32),
            pltpu.VMEM((512, 512), F32),
            pltpu.VMEM((256, MEL), F32),
            pltpu.VMEM((328, 128), F32),
            pltpu.VMEM((8, 128), F32),
            pltpu.VMEM((2, 32, 384), BF16),
            pltpu.VMEM((2, 32, 384), F32),
            pltpu.VMEM((32, 384), BF16),
            pltpu.VMEM((48, 384), F32),
            pltpu.VMEM((6, Z, 4, 16, 384), BF16),
            pltpu.VMEM((896, 384), F32),
            pltpu.VMEM((Z, 96, 384), BF16),
            pltpu.VMEM((Z, 96, 384), BF16),
            pltpu.VMEM((Z, 96, 384), BF16),
            pltpu.VMEM((8, 8, 128), F32),
            pltpu.VMEM((8, 8, 128), F32),
            pltpu.VMEM((4, 264, 128), F32),
            pltpu.VMEM((4, 264, 128), F32),
            pltpu.VMEM((4, 256, 384), BF16),
            pltpu.VMEM((256, 1536), BF16),
            pltpu.VMEM((288, 384), BF16),
            pltpu.VMEM((288, 384), F32),
            pltpu.VMEM((256, 384), BF16),
            pltpu.VMEM((4, 256, 384), BF16),
            pltpu.VMEM((4, 256, 384), BF16),
            dma((4,)),
            dma, dma,
            dma, dma,
            dma((8,)), dma((8,)),
            dma((8,)), dma((8,)),
            dma((4,)), dma((4,)),
            dma((4,)), dma,
            dma((4,)), dma((4,)),
            dma((2,)), dma((2,)),
            dma((4,)), dma((4,)),
            dma((3, Z)), dma((3, Z)),
            dma((3, 4)), dma((3, 4)),
            dma((3,)), dma((3,)),
        ],
        compiler_params=pltpu.CompilerParams(
            collective_id=0, has_side_effects=True, vmem_limit_bytes=60 * 1024 * 1024
        ),
    )(
        lengths,
        sub_weight,
        value_weight,
        gate_weight,
        out_weight.T,
        waveform.reshape(320, 128),
        depth_kernel,
        norm_scale,
        norm_shift,
        jnp.asarray(fourier_table()),
        jnp.asarray(mel_filters()),
    )
    return encoded[None]


def solution(mesh):
    placed = (
        P("dp", ("tm", "mp")),
        P("dp"),
        P(("dp", "tm"), "mp"),
        P(("dp", "tm"), "mp"),
        P(("dp", "tm"), "mp"),
        P("mp", ("dp", "tm")),
        P(None, "mp"),
        P("mp"),
        P("mp"),
    )
    return jax.shard_map(
        shards, mesh=mesh, in_specs=placed, out_specs=P("dp", "tm", "mp"), check_vma=False
    )
```

time: 107 us -> 87.1 us (0.81)
  the two profiles are of different devices: /device:TPU:1 before, /device:TPU:23 now
where the time goes in v2:
time: 87.1 us; the launch traced here: 86.9 us
  Pallas kernels  84.6 us (97%)
  local copies, waits for them, and re-layouts  1.62 us (2%)
    pallas_call x1, Pallas kernels, shards(): pl.pallas_call(kernel, out_shape=jax.ShapeDtypeStruct((256, 384), BF16),...  84.6 us

profile of v2, /device:TPU:23, one launch (start us, length us, event | category | flops | bytes accessed | tf_op | source)
XLA Modules:
  0.0 86.9 jit_solution(5361342547407873306)
XLA Ops:
  0.7 84.6 %shard_map.109 = bf16[256,384]{1,0:T(8,128)(2,1)} custom-call(s32[1]{0:T(128)S(6)} %copy.13.len_ref, bf16[7,384]{1,0:T(8,128)(2,1)} %subw.1, bf16[12,384]{1,0:T(8,128)(2,1)} %valw.1, bf16[12,384]{1,0:T(8,128)(2,1)} %gatw.1, bf16[12,384]{1,0:T(8,128)(2,1)} %bitcast.5, f32[320,128]{1,0:T(8,128)} %bitcast.4, f32[31,384]{1,0:T(8,128)} %dk_hbm.1, f32[384]{0:T(512)} %scale.1, ...), custom_call_target="tpu_custom_call" | custom-call | tf_op jit(solution)/shard_map/pallas_call | solution.py:475
  85.3 1.6 %copy.14 = bf16[1,256,384]{2,1,0:T(8,128)(2,1)} copy(bf16[1,256,384]{2,1,0:T(8,128)(2,1)} %bitcast.3) | data formatting | bytes 393216

commit v3 on v2

--- a/solution.py
+++ b/solution.py
@@ -57,7 +57,7 @@
 def kernel(
     len_ref, subw, valw, gatw, outw, wav_hbm, dk_hbm, scale, shift, table_hbm, filters_hbm,
     out_ref,
-    wav, dk, table, filters, wbuf, halo, pack, packf, got, own48, w, sf, vw, gw, ow,
+    wav, dk, table, filters, wbuf, halo, lg, pack, packf, got, own48, w, sf, vw, gw, ow,
     ma, mb, le, nmf, feats, normed, gp, gf, act, ps, rs,
     in_s, h_s, h_r, c_s, c_r, ma_s, ma_r, mb_s, mb_r, le_s, le_r, lh_s, lh_r, ag_s, ag_r,
     gh_s, gh_r, rs_s, rs_r, z_s, z_r, x_s, x_r, sib_s, sib_r,
@@ -70,7 +70,6 @@
     x = q // 2
     core = tm % 2
     z = z_hi * 8 + dp
-    slab = dp * 2 + z_hi
     length = len_ref[0]
     seg = tm * 4 + mp
     tm_up, tm_down = (tm + 1) % 16, (tm + 15) % 16
@@ -120,22 +119,46 @@
     packf[1, 12:24, :] = gatw[...].astype(F32)
     pack[...] = packf[...].astype(BF16)
 
+    position = (
+        seg * 40960
+        + lax.broadcasted_iota(jnp.int32, (328, 128), 0) * 128
+        + lax.broadcasted_iota(jnp.int32, (328, 128), 1)
+    )
+
+    def log_mel(start, count, steps):
+        wide = jnp.concatenate(
+            [wbuf[pl.ds(5 * start + c, count, stride=5), :] for c in range(7)], axis=1
+        )
+        frames = jnp.concatenate(
+            [
+                (pltpu.roll(wide, 896 - HOP * j, 1) if j else wide)[:, :512]
+                for j in steps
+            ],
+            axis=0,
+        )
+        spectrum = exact_dot(frames, table[...])
+        power = (
+            spectrum[:, :256] * spectrum[:, :256] + spectrum[:, 256:] * spectrum[:, 256:]
+        )
+        energy = jnp.log(exact_dot(power, filters[...]) + 1e-06)
+        for k, j in enumerate(steps):
+            lg[j, start : start + count, :] = energy[k * count : k * count + count]
+
+    loads[0].wait()
+    wbuf[0:320] = jnp.where(position[:320] < length, wav[...], 0.0)
+    wbuf[320:328] = jnp.zeros((8, 128), F32)
+    loads[1].wait()
+    loads[2].wait()
+    log_mel(0, 64, range(STRIDE))
+
     pl.semaphore_wait(barrier, 15 + 7 + 3 + 3 + 8)
 
     swap = remote(pack.at[1 - core], got, c_s, c_r, tm=twin)
     swap.start()
-    loads[0].wait()
     prev_mp = (mp + 3) % 4
     prev_tm = (tm + 15 + (mp + 3) // 4) % 16
     halo_copy = remote(wav.at[0:8], halo, h_s, h_r, tm=prev_tm, mp=prev_mp)
     halo_copy.start()
-
-    position = (
-        seg * 40960
-        + lax.broadcasted_iota(jnp.int32, (328, 128), 0) * 128
-        + lax.broadcasted_iota(jnp.int32, (328, 128), 1)
-    )
-    wbuf[0:320] = jnp.where(position[:320] < length, wav[...], 0.0)
 
     swap.wait_recv()
     mine, other = packf[core], got[...].astype(F32)
@@ -158,73 +181,96 @@
         own48[24:36] = first[12:24]
         own48[36:48] = second[12:24]
 
-    batch = [core * 3 + j for j in range(3)]
-    for j in range(3):
-        w[batch[j], slab, x] = own48[16 * j : 16 * j + 16].astype(BF16)
-
-    def push_z(j, i):
-        ref = w.at[batch[j], slab, x]
-        return remote(ref, ref, z_s.at[j, i], z_r.at[j, i], **along_z(i))
-
-    def from_z(j, i):
+    def on(which):
+        return pl.when(core == which)
+
+    for c in range(2):
+        @on(c)
+        def _(c=c):
+            for j in range(3):
+                w[3 * c + j, z % 4, z // 4, x] = own48[16 * j : 16 * j + 16].astype(BF16)
+
+    def push_z(b, i):
+        ref = w.at[b, z % 4, z // 4, x]
+        return remote(ref, ref, z_s.at[b, i], z_r.at[b, i], **along_z(i))
+
+    def from_z(b, i):
         at = (z + Z - i) % Z
-        ref = w.at[batch[j], (at % 8) * 2 + at // 8, x]
-        return remote(ref, ref, z_s.at[j, i], z_r.at[j, i], **along_z(i))
-
-    def push_x(j, i):
-        ref = w.at[batch[j], :, x]
+        ref = w.at[b, at % 4, at // 4, x]
+        return remote(ref, ref, z_s.at[b, i], z_r.at[b, i], **along_z(i))
+
+    near = {1: pl.ds(0, 4), 15: pl.ds(0, 4), 2: pl.ds(0, 2), 14: pl.ds(2, 2)}
+
+    def push_near(b, i):
+        ref = w.at[b, z % 4, near[i], x]
+        return remote(ref, ref, z_s.at[b, i], z_r.at[b, i], **along_z(i))
+
+    def from_near(b, i):
+        ref = w.at[b, (z + Z - i) % 4, near[i], x]
+        return remote(ref, ref, z_s.at[b, i], z_r.at[b, i], **along_z(i))
+
+    def column(b, i):
+        return w.at[b, :, :, (x + 4 - i) % 4]
+
+    def push_x(b, i):
         return remote(
-            ref, ref, x_s.at[j, i], x_r.at[j, i],
+            column(b, 0), column(b, 0), x_s.at[b, i], x_r.at[b, i],
             tm=z_hi * 8 + ((x + i) % 4) * 2 + core,
         )
 
-    def from_x(j, i):
-        ref = w.at[batch[j], :, (x + 4 - i) % 4]
+    def from_x(b, i):
         return remote(
-            ref, ref, x_s.at[j, i], x_r.at[j, i],
+            column(b, i), column(b, i), x_s.at[b, i], x_r.at[b, i],
             tm=z_hi * 8 + ((x + i) % 4) * 2 + core,
         )
 
-    def push_twin(j):
-        ref = w.at[batch[j]]
-        return remote(ref, ref, sib_s.at[j], sib_r.at[j], tm=twin)
-
-    def from_twin(j):
-        ref = w.at[(1 - core) * 3 + j]
-        return remote(ref, ref, sib_s.at[j], sib_r.at[j], tm=twin)
-
-    def send_z(j):
-        for i in (8, 7, 9, 6, 10, 5, 11, 4, 12, 3, 13, 2, 14, 1, 15):
-            push_z(j, i).start()
-
-    def send_x(j):
-        for i in range(1, Z):
-            from_z(j, i).wait_recv()
+    def twin_copy(b, i):
+        return remote(column(b, i), column(b, i), sib_s.at[b, i], sib_r.at[b, i], tm=twin)
+
+    FAR = (8, 4, 12)
+    AHEAD = (8, 7, 9, 6, 10, 5, 11, 4, 12, 3, 13, 2, 14, 1, 15)
+
+    def send_far(b):
+        for i in FAR:
+            push_z(b, i).start()
+
+    def send_near(b):
+        for i in FAR:
+            from_z(b, i).wait_recv()
+        for i in near:
+            push_near(b, i).start()
+
+    def send_x(b):
+        for i in near if b else range(1, Z):
+            (from_near if b else from_z)(b, i).wait_recv()
         for i in (2, 1, 3):
-            push_x(j, i).start()
-
-    def send_twin(j):
-        for i in range(1, 4):
-            from_x(j, i).wait_recv()
-        push_twin(j).start()
-
-    send_z(0)
+            push_x(b, i).start()
+        twin_copy(b, 0).start()
+
+    def send_twin(b):
+        for i in (1, 3, 2):
+            from_x(b, i).wait_recv()
+            twin_copy(b, i).start()
+
+    def from_twin(b):
+        for i in (0, 1, 3, 2):
+            twin_copy(b, i).wait_recv()
+
+    @on(0)
+    def _():
+        for i in AHEAD:
+            push_z(0, i).start()
+
+    @on(1)
+    def _():
+        send_far(3)
 
     halo_copy.wait_recv()
     wbuf[320:328] = jnp.where(position[320:328] < length, halo[...], 0.0)
-    wide = jnp.concatenate([wbuf[pl.ds(c, 64, stride=5), :] for c in range(7)], axis=1)
-    frames = jnp.concatenate(
-        [wide[:, :512]]
-        + [pltpu.roll(wide, 896 - HOP * j, 1)[:, :512] for j in range(1, STRIDE)],
-        axis=0,
-    )
-    loads[1].wait()
-    loads[2].wait()
-    spectrum = exact_dot(frames, table[...])
-    power = spectrum[:, :256] * spectrum[:, :256] + spectrum[:, 256:] * spectrum[:, 256:]
-    log_energy = jnp.log(exact_dot(power, filters[...]) + 1e-06)
+    log_mel(56, 8, (2, 3))
     row = lax.broadcasted_iota(jnp.int32, (256, MEL), 0)
     valid_mel = seg * 256 + (row % 64) * 4 + row // 64 < length // HOP
+    log_energy = jnp.concatenate([lg[j] for j in range(STRIDE)], axis=0)
     kept = jnp.where(valid_mel, log_energy, 0.0)
     ma[q] = jnp.concatenate(
         [
@@ -269,6 +315,11 @@
 
     for i in (2, 1, 3):
         mel_gather(i).start()
+
+    @on(1)
+    def _():
+        send_near(3)
+
     for i in range(1, 8):
         moments_a(i).wait_recv()
     total = ma[0]
@@ -286,9 +337,16 @@
 
     for i in (4, 5, 6, 7, 3, 2, 1):
         moments_b(i).start()
-    send_z(1)
-    send_x(0)
-    send_z(2)
+
+    @on(0)
+    def _():
+        send_x(0)
+
+    @on(1)
+    def _():
+        send_far(4)
+        send_far(5)
+
     for i in range(1, 8):
         moments_b(i).wait_recv()
     total = mb[0]
@@ -306,13 +364,25 @@
         known = (time >= 0) & (time * 4 + j < length // HOP)
         nmf[j] = jnp.where(known, (le[j] - mel_mean) * mel_scale, 0.0)
 
-    send_x(1)
-    send_twin(0)
-    from_twin(0).wait_recv()
+    @on(0)
+    def _():
+        send_twin(0)
+        send_far(1)
+        send_far(2)
+
+    @on(1)
+    def _():
+        send_x(3)
+        send_near(4)
+        send_near(5)
+        from_twin(0)
 
     for s in range(Z):
         for i in range(4):
-            sf[56 * s + 14 * i : 56 * s + 14 * i + 14, :] = w[0, s, i].astype(F32)[0:14]
+            at = (s % 2) * 8 + s // 2
+            sf[56 * s + 14 * i : 56 * s + 14 * i + 14, :] = w[0, at % 4, at // 4, i].astype(
+                F32
+            )[0:14]
     stacked = jnp.concatenate(
         [nmf[j, 7:263] for j in range(1, STRIDE)] + [nmf[j, 8:264] for j in range(STRIDE)],
         axis=1,
@@ -332,9 +402,20 @@
 
     for i in (2, 1, 3):
         gather(i).start()
-    send_x(2)
-    send_twin(1)
-    send_twin(2)
+
+    @on(0)
+    def _():
+        send_near(1)
+        send_near(2)
+        send_x(1)
+        send_x(2)
+
+    @on(1)
+    def _():
+        send_x(4)
+        send_x(5)
+        for b in (3, 4, 5):
+            send_twin(b)
 
     for i in range(1, 4):
         gather_in(i).wait_recv()
@@ -347,14 +428,19 @@
         spread = jnp.mean(centered * centered, axis=1, keepdims=True)
         normed[rows, :] = (centered * lax.rsqrt(spread + 1e-05)).astype(BF16)
 
-    from_twin(1).wait_recv()
-    from_twin(2).wait_recv()
+    @on(0)
+    def _():
+        for b in (3, 4, 5):
+            from_twin(b)
 
     @pl.loop(0, Z)
     def _(s):
         value, gate = [], []
+        at = (s % 2) * 8 + s // 2
         for i in range(4):
-            top, middle, bottom = (w[b, s, i].astype(F32) for b in (3, 4, 5))
+            top, middle, bottom = (
+                w[b, at % 4, at // 4, i].astype(F32) for b in (3, 4, 5)
+            )
             value += [top, middle[0:8]]
             gate += [middle[8:16], bottom]
         vw[s] = jnp.concatenate(value, axis=0).astype(BF16)
@@ -415,11 +501,25 @@
     def _(b):
         depthwise((b // 3) * 3, b % 3)
 
+    @on(0)
+    def _():
+        send_twin(1)
+        send_twin(2)
+
+    @on(1)
+    def _():
+        from_twin(1)
+        from_twin(2)
+
     @pl.loop(0, Z)
     def _(s):
         rows = []
+        at = (s % 2) * 8 + s // 2
         for i in range(4):
-            rows += [w[1, s, i].astype(F32), w[2, s, i].astype(F32)[0:8]]
+            rows += [
+                w[1, at % 4, at // 4, i].astype(F32),
+                w[2, at % 4, at // 4, i].astype(F32)[0:8],
+            ]
         ow[s] = jnp.concatenate(rows, axis=0).astype(BF16)
 
     def partial(g):
@@ -457,12 +557,19 @@
 
     to_next.wait_send()
     to_prev.wait_send()
-    for j in range(3):
-        for i in range(1, Z):
-            push_z(j, i).wait_send()
-        for i in range(1, 4):
-            push_x(j, i).wait_send()
-        push_twin(j).wait_send()
+
+    for c in range(2):
+        @on(c)
+        def _(c=c):
+            for b in range(3 * c, 3 * c + 3):
+                for i in FAR if b else AHEAD:
+                    push_z(b, i).wait_send()
+                for i in near if b else ():
+                    push_near(b, i).wait_send()
+                for i in range(1, 4):
+                    push_x(b, i).wait_send()
+                for i in range(4):
+                    twin_copy(b, i).wait_send()
 
 
 def shards(
@@ -484,11 +591,12 @@
             pltpu.VMEM((256, MEL), F32),
             pltpu.VMEM((328, 128), F32),
             pltpu.VMEM((8, 128), F32),
+            pltpu.VMEM((4, 64, 128), F32),
             pltpu.VMEM((2, 32, 384), BF16),
             pltpu.VMEM((2, 32, 384), F32),
             pltpu.VMEM((32, 384), BF16),
             pltpu.VMEM((48, 384), F32),
-            pltpu.VMEM((6, Z, 4, 16, 384), BF16),
+            pltpu.VMEM((6, 4, 4, 4, 16, 384), BF16),
             pltpu.VMEM((896, 384), F32),
             pltpu.VMEM((Z, 96, 384), BF16),
             pltpu.VMEM((Z, 96, 384), BF16),
@@ -514,9 +622,9 @@
             dma((4,)), dma((4,)),
             dma((2,)), dma((2,)),
             dma((4,)), dma((4,)),
-            dma((3, Z)), dma((3, Z)),
-            dma((3, 4)), dma((3, 4)),
-            dma((3,)), dma((3,)),
+            dma((6, Z)), dma((6, Z)),
+            dma((6, 4)), dma((6, 4)),
+            dma((6, 4)), dma((6, 4)),
         ],
         compiler_params=pltpu.CompilerParams(
             collective_id=0, has_side_effects=True, vmem_limit_bytes=60 * 1024 * 1024

time: 87.1 us -> 86.7 us (level)
  the two profiles are of different devices: /device:TPU:23 before, /device:TPU:1 now
where the time goes in v3:
time: 86.7 us; the launch traced here: 86.5 us
  Pallas kernels  84.2 us (97%)
  local copies, waits for them, and re-layouts  1.62 us (2%)
    pallas_call x1, Pallas kernels, shards(): pl.pallas_call(kernel, out_shape=jax.ShapeDtypeStruct((256, 384), BF16),...  84.2 us

profile of v3, /device:TPU:1, one launch (start us, length us, event | category | flops | bytes accessed | tf_op | source)
XLA Modules:
  0.0 86.5 jit_solution(2464882389146300726)
XLA Ops:
  0.7 84.2 %shard_map.109 = bf16[256,384]{1,0:T(8,128)(2,1)} custom-call(s32[1]{0:T(128)S(6)} %copy.13.len_ref, bf16[7,384]{1,0:T(8,128)(2,1)} %subw.1, bf16[12,384]{1,0:T(8,128)(2,1)} %valw.1, bf16[12,384]{1,0:T(8,128)(2,1)} %gatw.1, bf16[12,384]{1,0:T(8,128)(2,1)} %bitcast.5, f32[320,128]{1,0:T(8,128)} %bitcast.4, f32[31,384]{1,0:T(8,128)} %dk_hbm.1, f32[384]{0:T(512)} %scale.1, ...), custom_call_target="tpu_custom_call" | custom-call | tf_op jit(solution)/shard_map/pallas_call | solution.py:582
  84.8 1.6 %copy.14 = bf16[1,256,384]{2,1,0:T(8,128)(2,1)} copy(bf16[1,256,384]{2,1,0:T(8,128)(2,1)} %bitcast.3) | data formatting | bytes 393216

commit v4 on v3

--- a/solution.py
+++ b/solution.py
@@ -60,7 +60,7 @@
     wav, dk, table, filters, wbuf, halo, lg, pack, packf, got, own48, w, sf, vw, gw, ow,
     ma, mb, le, nmf, feats, normed, gp, gf, act, ps, rs,
     in_s, h_s, h_r, c_s, c_r, ma_s, ma_r, mb_s, mb_r, le_s, le_r, lh_s, lh_r, ag_s, ag_r,
-    gh_s, gh_r, rs_s, rs_r, z_s, z_r, x_s, x_r, sib_s, sib_r,
+    gh_s, gh_r, rs_s, rs_r, z_s, far_r, near_r, x_s, x_r, sib_s, sib_r,
 ):
     dp = lax.axis_index("dp")
     tm = lax.axis_index("tm")
@@ -80,6 +80,12 @@
             src_ref=src, dst_ref=dst, send_sem=ssem, recv_sem=rsem,
             device_id=dev, device_id_type=pl.DeviceIdType.MESH,
         )
+
+    def arrived(ref, rsem):
+        remote(ref, ref, c_s, rsem, tm=twin).wait_recv()
+
+    def left(ref, ssem):
+        remote(ref, ref, ssem, c_r, tm=twin).wait_send()
 
     loads = [
         pltpu.make_async_copy(there, here, in_s.at[i])
@@ -190,80 +196,72 @@
             for j in range(3):
                 w[3 * c + j, z % 4, z // 4, x] = own48[16 * j : 16 * j + 16].astype(BF16)
 
-    def push_z(b, i):
-        ref = w.at[b, z % 4, z // 4, x]
-        return remote(ref, ref, z_s.at[b, i], z_r.at[b, i], **along_z(i))
-
-    def from_z(b, i):
-        at = (z + Z - i) % Z
-        ref = w.at[b, at % 4, at // 4, x]
-        return remote(ref, ref, z_s.at[b, i], z_r.at[b, i], **along_z(i))
-
-    near = {1: pl.ds(0, 4), 15: pl.ds(0, 4), 2: pl.ds(0, 2), 14: pl.ds(2, 2)}
-
-    def push_near(b, i):
-        ref = w.at[b, z % 4, near[i], x]
-        return remote(ref, ref, z_s.at[b, i], z_r.at[b, i], **along_z(i))
-
-    def from_near(b, i):
-        ref = w.at[b, (z + Z - i) % 4, near[i], x]
-        return remote(ref, ref, z_s.at[b, i], z_r.at[b, i], **along_z(i))
+    def push(ref, ssem, rsem, **dev):
+        remote(ref, ref, ssem, rsem, **dev).start()
+
+    FAR = (8, 4, 12)
+    AHEAD = (8, 7, 9, 6, 10, 5, 11, 4, 12, 3, 13, 2, 14, 1, 15)
+    NEAR = {1: pl.ds(0, 4), 15: pl.ds(0, 4), 2: pl.ds(0, 2), 14: pl.ds(2, 2)}
+
+    def own_tile(b):
+        return w.at[b, z % 4, z // 4] if b == 2 else w.at[b, z % 4, z // 4, x]
+
+    def own_class(b, part):
+        return w.at[b, z % 4, part] if b == 2 else w.at[b, z % 4, part, x]
+
+    def tiles(b, n):
+        if n == 15:
+            return vw.at[pl.ds(0, 15), pl.ds(0, 16)]
+        if n == 3:
+            return w.at[b, 0, 0, pl.ds(0, 3)]
+        if n == 12:
+            return w.at[b, 0, pl.ds(0, 3)]
+        return w.at[b, pl.ds(0, n // 16)]
+
+    def along_x(i):
+        return {"tm": z_hi * 8 + ((x + i) % 4) * 2 + core}
+
+    def send_far(b):
+        for i in FAR if b else AHEAD:
+            push(own_tile(b), z_s.at[b], far_r.at[b], **along_z(i))
+
+    def send_near(b):
+        arrived(tiles(b, 12 if b == 2 else 3), far_r.at[b])
+        for i, part in NEAR.items():
+            push(own_class(b, part), z_s.at[6 if b == 2 else b], near_r.at[b], **along_z(i))
 
     def column(b, i):
         return w.at[b, :, :, (x + 4 - i) % 4]
 
-    def push_x(b, i):
-        return remote(
-            column(b, 0), column(b, 0), x_s.at[b, i], x_r.at[b, i],
-            tm=z_hi * 8 + ((x + i) % 4) * 2 + core,
-        )
-
-    def from_x(b, i):
-        return remote(
-            column(b, i), column(b, i), x_s.at[b, i], x_r.at[b, i],
-            tm=z_hi * 8 + ((x + i) % 4) * 2 + core,
-        )
-
-    def twin_copy(b, i):
-        return remote(column(b, i), column(b, i), sib_s.at[b, i], sib_r.at[b, i], tm=twin)
-
-    FAR = (8, 4, 12)
-    AHEAD = (8, 7, 9, 6, 10, 5, 11, 4, 12, 3, 13, 2, 14, 1, 15)
-
-    def send_far(b):
-        for i in FAR:
-            push_z(b, i).start()
-
-    def send_near(b):
-        for i in FAR:
-            from_z(b, i).wait_recv()
-        for i in near:
-            push_near(b, i).start()
-
     def send_x(b):
-        for i in near if b else range(1, Z):
-            (from_near if b else from_z)(b, i).wait_recv()
+        if b:
+            arrived(tiles(b, 12), near_r.at[b])
+        else:
+            arrived(tiles(b, 15), far_r.at[b])
         for i in (2, 1, 3):
-            push_x(b, i).start()
-        twin_copy(b, 0).start()
+            push(column(b, 0), x_s.at[b], x_r.at[b], **along_x(i))
+        push(column(b, 0), sib_s.at[b], sib_r.at[b], tm=twin)
 
     def send_twin(b):
+        arrived(tiles(b, 48), x_r.at[b])
         for i in (1, 3, 2):
-            from_x(b, i).wait_recv()
-            twin_copy(b, i).start()
+            push(column(b, i), sib_s.at[b], sib_r.at[b], tm=twin)
+
+    def first_x():
+        ref = w.at[2, z % 4, z // 4, x]
+        for i in (2, 1, 3):
+            push(ref, x_s.at[2], x_r.at[2], **along_x(i))
+
+    def far_2():
+        arrived(tiles(2, 3), x_r.at[2])
+        send_far(2)
+
+    def twin_2():
+        arrived(tiles(2, 48), near_r.at[2])
+        push(w.at[2], sib_s.at[2], sib_r.at[2], tm=twin)
 
     def from_twin(b):
-        for i in (0, 1, 3, 2):
-            twin_copy(b, i).wait_recv()
-
-    @on(0)
-    def _():
-        for i in AHEAD:
-            push_z(0, i).start()
-
-    @on(1)
-    def _():
-        send_far(3)
+        arrived(w.at[b], sib_r.at[b])
 
     halo_copy.wait_recv()
     wbuf[320:328] = jnp.where(position[320:328] < length, halo[...], 0.0)
@@ -272,7 +270,8 @@
     valid_mel = seg * 256 + (row % 64) * 4 + row // 64 < length // HOP
     log_energy = jnp.concatenate([lg[j] for j in range(STRIDE)], axis=0)
     kept = jnp.where(valid_mel, log_energy, 0.0)
-    ma[q] = jnp.concatenate(
+    place = z_hi * 4 + mp
+    ma[place] = jnp.concatenate(
         [
             jnp.sum(kept, axis=0, keepdims=True),
             jnp.sum(kept * kept, axis=0, keepdims=True),
@@ -281,74 +280,56 @@
         axis=0,
     )
 
-    def moments_a(i):
-        return remote(
-            ma.at[q], ma.at[q], ma_s.at[i], ma_r.at[i], tm=z_hi * 8 + (q + i) % 8
-        )
-
-    for i in range(1, 8):
-        moments_a(i).start()
+    for i in (4, 5, 6, 7, 3, 2, 1):
+        away = (place + i) % 8
+        push(ma.at[place], ma_s, ma_r, tm=(away // 4) * 8 + q, mp=away % 4)
+
+    @on(0)
+    def _():
+        send_far(0)
+        first_x()
+
+    @on(1)
+    def _():
+        send_far(3)
+        send_far(4)
+        send_far(5)
 
     own = pl.ds(pl.multiple_of(8 + mp * 64, 8), 64)
     for j in range(STRIDE):
         le[j, own, :] = log_energy[j * 64 : j * 64 + 64]
 
-    def mel_gather(i):
-        ref = le.at[:, own, :]
-        return remote(ref, ref, le_s.at[i], le_r.at[i], mp=(mp + i) % 4)
-
-    def mel_gather_in(i):
-        there = pl.ds(pl.multiple_of(8 + ((mp + 4 - i) % 4) * 64, 8), 64)
-        ref = le.at[:, there, :]
-        return remote(ref, ref, le_s.at[i], le_r.at[i], mp=(mp + i) % 4)
-
-    def mel_halo(i):
-        return remote(
-            le.at[:, pl.ds(256, 8), :], le.at[:, pl.ds(0, 8), :],
-            lh_s.at[i], lh_r, tm=tm_up, mp=(mp + i) % 4,
-        )
+    ours = le.at[:, own, :]
+    next_halo = le.at[:, pl.ds(256, 8), :], le.at[:, pl.ds(0, 8), :]
 
     @pl.when(mp == 3)
     def _():
         for i in range(4):
-            mel_halo(i).start()
+            remote(*next_halo, lh_s, lh_r, tm=tm_up, mp=(mp + i) % 4).start()
 
     for i in (2, 1, 3):
-        mel_gather(i).start()
-
-    @on(1)
-    def _():
-        send_near(3)
-
-    for i in range(1, 8):
-        moments_a(i).wait_recv()
+        push(ours, le_s, le_r, mp=(mp + i) % 4)
+    arrived(ma.at[pl.ds(0, 7)], ma_r)
     total = ma[0]
     for i in range(1, 8):
         total = total + ma[i]
-    place = z_hi * 4 + mp
-    mb[place] = total
-
-    def moments_b(i):
-        away = (place + i) % 8
-        return remote(
-            mb.at[place], mb.at[place], mb_s.at[i], mb_r.at[i],
-            tm=(away // 4) * 8 + q, mp=away % 4,
-        )
-
-    for i in (4, 5, 6, 7, 3, 2, 1):
-        moments_b(i).start()
+    mb[q] = total
+    for i in range(1, 8):
+        push(mb.at[q], mb_s, mb_r, tm=z_hi * 8 + (q + i) % 8)
 
     @on(0)
     def _():
         send_x(0)
+        send_far(1)
+        far_2()
 
     @on(1)
     def _():
-        send_far(4)
-        send_far(5)
-
-    for i in range(1, 8):
-        moments_b(i).wait_recv()
+        send_near(3)
+        send_near(4)
+        send_near(5)
+
+    arrived(mb.at[pl.ds(0, 7)], mb_r)
     total = mb[0]
     for i in range(1, 8):
         total = total + mb[i]
@@ -356,9 +337,8 @@
     mel_mean = total[0:1] / count
     mel_var = total[1:2] / count - mel_mean * mel_mean
     mel_scale = lax.rsqrt(mel_var + 1e-05)
-    for i in range(1, 4):
-        mel_gather_in(i).wait_recv()
-    mel_halo(0).wait_recv()
+    arrived(le.at[:, pl.ds(0, 192), :], le_r)
+    arrived(le.at[:, pl.ds(0, 8), :], lh_r)
     time = tm * 256 - 8 + lax.broadcasted_iota(jnp.int32, (264, MEL), 0)
     for j in range(STRIDE):
         known = (time >= 0) & (time * 4 + j < length // HOP)
@@ -367,14 +347,12 @@
     @on(0)
     def _():
         send_twin(0)
-        send_far(1)
-        send_far(2)
 
     @on(1)
     def _():
         send_x(3)
-        send_near(4)
-        send_near(5)
+        send_x(4)
+        send_x(5)
         from_twin(0)
 
     for s in range(Z):
@@ -391,34 +369,21 @@
         stacked, sf[...].astype(BF16), preferred_element_type=F32
     ).astype(BF16)
 
-    def gather(i):
-        return remote(
-            feats.at[mp], feats.at[mp], ag_s.at[i], ag_r.at[i], mp=(mp + i) % 4
-        )
-
-    def gather_in(i):
-        ref = feats.at[(mp + 4 - i) % 4]
-        return remote(ref, ref, ag_s.at[i], ag_r.at[i], mp=(mp + i) % 4)
-
     for i in (2, 1, 3):
-        gather(i).start()
+        push(feats.at[mp], ag_s, ag_r, mp=(mp + i) % 4)
 
     @on(0)
     def _():
         send_near(1)
         send_near(2)
         send_x(1)
-        send_x(2)
 
     @on(1)
     def _():
-        send_x(4)
-        send_x(5)
         for b in (3, 4, 5):
             send_twin(b)
 
-    for i in range(1, 4):
-        gather_in(i).wait_recv()
+    arrived(feats.at[pl.ds(0, 3)], ag_r)
 
     @pl.loop(0, 8)
     def _(b):
@@ -492,24 +457,15 @@
     def _(b):
         depthwise(b // 3 + 1, b % 3)
 
-    to_next.wait_recv()
-    to_prev.wait_recv()
-    gf[0:16, :] = jnp.where(tm == 0, 0.0, gp[0:16, :].astype(F32))
-    gf[272:288, :] = jnp.where(tm == 15, 0.0, gp[272:288, :].astype(F32))
-
-    @pl.loop(0, 6)
-    def _(b):
-        depthwise((b // 3) * 3, b % 3)
-
     @on(0)
     def _():
+        twin_2()
         send_twin(1)
-        send_twin(2)
 
     @on(1)
     def _():
+        from_twin(2)
         from_twin(1)
-        from_twin(2)
 
     @pl.loop(0, Z)
     def _(s):
@@ -522,38 +478,56 @@
             ]
         ow[s] = jnp.concatenate(rows, axis=0).astype(BF16)
 
-    def partial(g):
+    def partial(rows, g):
         block = ow[pl.ds(g * 4, 4)].reshape(384, 384)
         return lax.dot_general(
-            act[...], block, NT, preferred_element_type=F32
+            rows, block, NT, preferred_element_type=F32
         ).astype(BF16)
 
-    def scatter(i):
-        return remote(ps.at[i], rs.at[i], rs_s.at[i], rs_r.at[i], mp=(mp + i) % 4)
-
+    def scatter(i, start, rows):
+        part = pl.ds(start, rows)
+        remote(
+            ps.at[i, part], rs.at[i, part], rs_s, rs_r, mp=(mp + i) % 4
+        ).start()
+
+    inner = act[64:192, :]
     for i in (2, 1, 3):
-        ps[i] = partial((mp + i) % 4)
-        scatter(i).start()
-    summed = partial(mp).astype(F32)
+        ps[i, 64:192] = partial(inner, (mp + i) % 4)
+        scatter(i, 64, 128)
+
+    to_next.wait_recv()
+    to_prev.wait_recv()
+    gf[0:16, :] = jnp.where(tm == 0, 0.0, gp[0:16, :].astype(F32))
+    gf[272:288, :] = jnp.where(tm == 15, 0.0, gp[272:288, :].astype(F32))
+
+    @pl.loop(0, 6)
+    def _(b):
+        depthwise((b // 3) * 3, b % 3)
+
+    outer = jnp.concatenate([act[0:64, :], act[192:256, :]], axis=0)
+    for i in (2, 1, 3):
+        part = partial(outer, (mp + i) % 4)
+        ps[i, 0:64] = part[0:64]
+        ps[i, 192:256] = part[64:128]
+        scatter(i, 0, 64)
+        scatter(i, 192, 64)
+    summed = partial(act[...], mp).astype(F32)
+    arrived(rs.at[pl.ds(1, 3)], rs_r)
     for i in range(1, 4):
-        scatter(i).wait_recv()
         summed = summed + rs[i].astype(F32)
     out_ref[...] = jnp.where(valid, feats[mp].astype(F32) + summed, 0.0).astype(BF16)
 
     halo_copy.wait_send()
     swap.wait_send()
-    for i in range(1, 8):
-        moments_a(i).wait_send()
-        moments_b(i).wait_send()
-    for i in range(1, 4):
-        mel_gather(i).wait_send()
-        gather(i).wait_send()
-        scatter(i).wait_send()
+    left(ma.at[pl.ds(0, 7)], ma_s)
+    left(mb.at[pl.ds(0, 7)], mb_s)
+    left(le.at[:, pl.ds(0, 192), :], le_s)
+    left(feats.at[pl.ds(0, 3)], ag_s)
+    left(rs.at[pl.ds(1, 3)], rs_s)
 
     @pl.when(mp == 3)
     def _():
-        for i in range(4):
-            mel_halo(i).wait_send()
+        left(le.at[:, pl.ds(0, 32), :], lh_s)
 
     to_next.wait_send()
     to_prev.wait_send()
@@ -562,14 +536,14 @@
         @on(c)
         def _(c=c):
             for b in range(3 * c, 3 * c + 3):
-                for i in FAR if b else AHEAD:
-                    push_z(b, i).wait_send()
-                for i in near if b else ():
-                    push_near(b, i).wait_send()
-                for i in range(1, 4):
-                    push_x(b, i).wait_send()
-                for i in range(4):
-                    twin_copy(b, i).wait_send()
+                if b == 2:
+                    left(tiles(b, 12), z_s.at[b])
+                    left(tiles(b, 48), z_s.at[6])
+                    left(tiles(b, 3), x_s.at[b])
+                else:
+                    left(tiles(b, 15), z_s.at[b])
+                    left(tiles(b, 48), x_s.at[b])
+                left(w.at[b], sib_s.at[b])
 
 
 def shards(
@@ -581,7 +555,7 @@
     dma = pltpu.SemaphoreType.DMA
     encoded = pl.pallas_call(
         kernel,
-        out_shape=jax.ShapeDtypeStruct((256, 384), BF16),
+        out_shape=pltpu.VMEM((256, 384), BF16),
         in_specs=[pl.BlockSpec(memory_space=pltpu.SMEM)] + [vmem] * 4 + [hbm] * 2 + [vmem] * 2 + [hbm] * 2,
         out_specs=vmem,
         scratch_shapes=[
@@ -615,16 +589,16 @@
             dma((4,)),
             dma, dma,
             dma, dma,
-            dma((8,)), dma((8,)),
-            dma((8,)), dma((8,)),
-            dma((4,)), dma((4,)),
-            dma((4,)), dma,
-            dma((4,)), dma((4,)),
+            dma, dma,
+            dma, dma,
+            dma, dma,
+            dma, dma,
+            dma, dma,
             dma((2,)), dma((2,)),
-            dma((4,)), dma((4,)),
-            dma((6, Z)), dma((6, Z)),
-            dma((6, 4)), dma((6, 4)),
-            dma((6, 4)), dma((6, 4)),
+            dma, dma,
+            dma((7,)), dma((6,)), dma((6,)),
+            dma((6,)), dma((6,)),
+            dma((6,)), dma((6,)),
         ],
         compiler_params=pltpu.CompilerParams(
             collective_id=0, has_side_effects=True, vmem_limit_bytes=60 * 1024 * 1024

time: 86.7 us -> 79.9 us (0.922)
  Pallas kernels: 84.2 us -> 78.3 us
  local copies, waits for them, and re-layouts: 1.62 us -> 0.68 us
    pallas_call x1, Pallas kernels: 84.2 us -> 78.3 us  [shards(): pl.pallas_call(kernel, out_shape=pltpu.VMEM((256, 384), BF16), in_specs=[...]
    unnamed x1, local copies, waits for them, and re-layouts: 1.62 us -> 0.68 us
where the time goes in v4:
time: 79.9 us; the launch traced here: 79.7 us
  Pallas kernels  78.3 us (98%)
    pallas_call x1, Pallas kernels, shards(): pl.pallas_call(kernel, out_shape=pltpu.VMEM((256, 384), BF16), in_specs=[...  78.3 us

profile of v4, /device:TPU:1, one launch (start us, length us, event | category | flops | bytes accessed | tf_op | source)
XLA Modules:
  0.0 79.7 jit_solution(16497886206201526182)
XLA Ops:
  0.7 78.3 %shard_map.109 = bf16[256,384]{1,0:T(8,128)(2,1)S(1)} custom-call(s32[1]{0:T(128)S(6)} %copy.14.len_ref, bf16[7,384]{1,0:T(8,128)(2,1)} %subw.1, bf16[12,384]{1,0:T(8,128)(2,1)} %valw.1, bf16[12,384]{1,0:T(8,128)(2,1)} %gatw.1, bf16[12,384]{1,0:T(8,128)(2,1)} %bitcast.5, f32[320,128]{1,0:T(8,128)} %bitcast.4, f32[31,384]{1,0:T(8,128)} %dk_hbm.1, f32[384]{0:T(512)} %scale.1, ...), custom_call_target="tpu_custom_call" | custom-call | tf_op jit(solution)/shard_map/pallas_call | solution.py:556
  79.0 0.7 copy.13

commit v5 on v4

--- a/solution.py
+++ b/solution.py
@@ -200,18 +200,19 @@
         remote(ref, ref, ssem, rsem, **dev).start()
 
     FAR = (8, 4, 12)
-    AHEAD = (8, 7, 9, 6, 10, 5, 11, 4, 12, 3, 13, 2, 14, 1, 15)
+    CLOSE = (4, 12, 3, 13, 2, 14, 1, 15)
+    APART = (8, 7, 9, 6, 10, 5, 11)
     NEAR = {1: pl.ds(0, 4), 15: pl.ds(0, 4), 2: pl.ds(0, 2), 14: pl.ds(2, 2)}
 
     def own_tile(b):
-        return w.at[b, z % 4, z // 4] if b == 2 else w.at[b, z % 4, z // 4, x]
+        return w.at[b, z % 4, z // 4] if b == 5 else w.at[b, z % 4, z // 4, x]
 
     def own_class(b, part):
-        return w.at[b, z % 4, part] if b == 2 else w.at[b, z % 4, part, x]
+        return w.at[b, z % 4, part] if b == 5 else w.at[b, z % 4, part, x]
 
     def tiles(b, n):
-        if n == 15:
-            return vw.at[pl.ds(0, 15), pl.ds(0, 16)]
+        if n in (7, 8, 15):
+            return vw.at[pl.ds(0, n), pl.ds(0, 16)]
         if n == 3:
             return w.at[b, 0, 0, pl.ds(0, 3)]
         if n == 12:
@@ -222,22 +223,39 @@
         return {"tm": z_hi * 8 + ((x + i) % 4) * 2 + core}
 
     def send_far(b):
-        for i in FAR if b else AHEAD:
+        for i in FAR:
             push(own_tile(b), z_s.at[b], far_r.at[b], **along_z(i))
 
+    def send_all():
+        for i in CLOSE:
+            push(own_tile(0), z_s.at[0], near_r.at[0], **along_z(i))
+        for i in APART:
+            push(own_tile(0), z_s.at[0], far_r.at[0], **along_z(i))
+
+    def pass_on(offsets):
+        for i in offsets:
+            at = (z + Z - i) % Z
+            ref = w.at[0, at % 4, at // 4, x]
+            for k in (2, 1, 3):
+                push(ref, x_s.at[0], x_r.at[0], **along_x(k))
+
+    def all_over_x():
+        arrived(tiles(0, 8), near_r.at[0])
+        pass_on((0,) + CLOSE)
+        arrived(tiles(0, 7), far_r.at[0])
+        pass_on(APART)
+        push(column(0, 0), sib_s.at[0], sib_r.at[0], tm=twin)
+
     def send_near(b):
-        arrived(tiles(b, 12 if b == 2 else 3), far_r.at[b])
+        arrived(tiles(b, 12 if b == 5 else 3), far_r.at[b])
         for i, part in NEAR.items():
-            push(own_class(b, part), z_s.at[6 if b == 2 else b], near_r.at[b], **along_z(i))
+            push(own_class(b, part), z_s.at[6 if b == 5 else b], near_r.at[b], **along_z(i))
 
     def column(b, i):
         return w.at[b, :, :, (x + 4 - i) % 4]
 
     def send_x(b):
-        if b:
-            arrived(tiles(b, 12), near_r.at[b])
-        else:
-            arrived(tiles(b, 15), far_r.at[b])
+        arrived(tiles(b, 12), near_r.at[b])
         for i in (2, 1, 3):
             push(column(b, 0), x_s.at[b], x_r.at[b], **along_x(i))
         push(column(b, 0), sib_s.at[b], sib_r.at[b], tm=twin)
@@ -248,17 +266,17 @@
             push(column(b, i), sib_s.at[b], sib_r.at[b], tm=twin)
 
     def first_x():
-        ref = w.at[2, z % 4, z // 4, x]
+        ref = w.at[5, z % 4, z // 4, x]
         for i in (2, 1, 3):
-            push(ref, x_s.at[2], x_r.at[2], **along_x(i))
-
-    def far_2():
-        arrived(tiles(2, 3), x_r.at[2])
-        send_far(2)
-
-    def twin_2():
-        arrived(tiles(2, 48), near_r.at[2])
-        push(w.at[2], sib_s.at[2], sib_r.at[2], tm=twin)
+            push(ref, x_s.at[5], x_r.at[5], **along_x(i))
+
+    def far_5():
+        arrived(tiles(5, 3), x_r.at[5])
+        send_far(5)
+
+    def twin_5():
+        arrived(tiles(5, 48), near_r.at[5])
+        push(w.at[5], sib_s.at[5], sib_r.at[5], tm=twin)
 
     def from_twin(b):
         arrived(w.at[b], sib_r.at[b])
@@ -286,14 +304,13 @@
 
     @on(0)
     def _():
-        send_far(0)
+        send_all()
+
+    @on(1)
+    def _():
         first_x()
-
-    @on(1)
-    def _():
         send_far(3)
         send_far(4)
-        send_far(5)
 
     own = pl.ds(pl.multiple_of(8 + mp * 64, 8), 64)
     for j in range(STRIDE):
@@ -319,15 +336,13 @@
 
     @on(0)
     def _():
-        send_x(0)
-        send_far(1)
-        far_2()
+        all_over_x()
 
     @on(1)
     def _():
+        far_5()
         send_near(3)
         send_near(4)
-        send_near(5)
 
     arrived(mb.at[pl.ds(0, 7)], mb_r)
     total = mb[0]
@@ -346,13 +361,15 @@
 
     @on(0)
     def _():
+        send_far(1)
+        send_far(2)
         send_twin(0)
 
     @on(1)
     def _():
+        send_near(5)
         send_x(3)
         send_x(4)
-        send_x(5)
         from_twin(0)
 
     for s in range(Z):
@@ -377,15 +394,17 @@
         send_near(1)
         send_near(2)
         send_x(1)
+        send_x(2)
 
     @on(1)
     def _():
-        for b in (3, 4, 5):
-            send_twin(b)
+        twin_5()
+        send_twin(3)
+        send_twin(4)
 
     arrived(feats.at[pl.ds(0, 3)], ag_r)
 
-    @pl.loop(0, 8)
+    @pl.loop(0, 8, unroll=2)
     def _(b):
         rows = pl.ds(pl.multiple_of(b * 32, 32), 32)
         wide = jnp.concatenate([feats[g, rows, :] for g in range(4)], axis=1).astype(F32)
@@ -395,7 +414,7 @@
 
     @on(0)
     def _():
-        for b in (3, 4, 5):
+        for b in (5, 3, 4):
             from_twin(b)
 
     @pl.loop(0, Z)
@@ -459,13 +478,13 @@
 
     @on(0)
     def _():
-        twin_2()
         send_twin(1)
+        send_twin(2)
 
     @on(1)
     def _():
+        from_twin(1)
         from_twin(2)
-        from_twin(1)
 
     @pl.loop(0, Z)
     def _(s):
@@ -536,7 +555,7 @@
         @on(c)
         def _(c=c):
             for b in range(3 * c, 3 * c + 3):
-                if b == 2:
+                if b == 5:
                     left(tiles(b, 12), z_s.at[b])
                     left(tiles(b, 48), z_s.at[6])
                     left(tiles(b, 3), x_s.at[b])

time: 79.9 us -> 78.3 us (0.980)
  Pallas kernels: 78.3 us -> 76.1 us
    pallas_call x1, Pallas kernels: 78.3 us -> 76.1 us  [shards(): pl.pallas_call(kernel, out_shape=pltpu.VMEM((256, 384), BF16), in_specs=[...]
where the time goes in v5:
time: 78.3 us; the launch traced here: 77.5 us
  Pallas kernels  76.1 us (97%)
    pallas_call x1, Pallas kernels, shards(): pl.pallas_call(kernel, out_shape=pltpu.VMEM((256, 384), BF16), in_specs=[...  76.1 us

profile of v5, /device:TPU:1, one launch (start us, length us, event | category | flops | bytes accessed | tf_op | source)
XLA Modules:
  0.0 77.5 jit_solution(7368646272886134733)
XLA Ops:
  0.7 76.1 %shard_map.109 = bf16[256,384]{1,0:T(8,128)(2,1)S(1)} custom-call(s32[1]{0:T(128)S(6)} %copy.14.len_ref, bf16[7,384]{1,0:T(8,128)(2,1)} %subw.1, bf16[12,384]{1,0:T(8,128)(2,1)} %valw.1, bf16[12,384]{1,0:T(8,128)(2,1)} %gatw.1, bf16[12,384]{1,0:T(8,128)(2,1)} %bitcast.5, f32[320,128]{1,0:T(8,128)} %bitcast.4, f32[31,384]{1,0:T(8,128)} %dk_hbm.1, f32[384]{0:T(512)} %scale.1, ...), custom_call_target="tpu_custom_call" | custom-call | tf_op jit(solution)/shard_map/pallas_call | solution.py:575
  76.8 0.7 copy.13

commit v6 on v5

--- a/solution.py
+++ b/solution.py
@@ -226,9 +226,11 @@
         for i in FAR:
             push(own_tile(b), z_s.at[b], far_r.at[b], **along_z(i))
 
-    def send_all():
+    def send_close():
         for i in CLOSE:
             push(own_tile(0), z_s.at[0], near_r.at[0], **along_z(i))
+
+    def send_apart():
         for i in APART:
             push(own_tile(0), z_s.at[0], far_r.at[0], **along_z(i))
 
@@ -280,6 +282,10 @@
 
     def from_twin(b):
         arrived(w.at[b], sib_r.at[b])
+
+    @on(0)
+    def _():
+        send_close()
 
     halo_copy.wait_recv()
     wbuf[320:328] = jnp.where(position[320:328] < length, halo[...], 0.0)
@@ -304,7 +310,9 @@
 
     @on(0)
     def _():
-        send_all()
+        send_apart()
+        send_far(1)
+        send_far(2)
 
     @on(1)
     def _():
@@ -337,6 +345,8 @@
     @on(0)
     def _():
         all_over_x()
+        send_near(1)
+        send_near(2)
 
     @on(1)
     def _():
@@ -361,8 +371,6 @@
 
     @on(0)
     def _():
-        send_far(1)
-        send_far(2)
         send_twin(0)
 
     @on(1)
@@ -391,9 +399,9 @@
 
     @on(0)
     def _():
-        send_near(1)
-        send_near(2)
         send_x(1)
+        from_twin(5)
+        from_twin(3)
         send_x(2)
 
     @on(1)
@@ -414,8 +422,7 @@
 
     @on(0)
     def _():
-        for b in (5, 3, 4):
-            from_twin(b)
+        from_twin(4)
 
     @pl.loop(0, Z)
     def _(s):

time: 78.3 us -> 78 us (level)
  no operation moved by 1% of the time
where the time goes in v6:
time: 78 us; the launch traced here: 76.7 us
  Pallas kernels  75.4 us (97%)
    pallas_call x1, Pallas kernels, shards(): pl.pallas_call(kernel, out_shape=pltpu.VMEM((256, 384), BF16), in_specs=[...  75.4 us

profile of v6, /device:TPU:1, one launch (start us, length us, event | category | flops | bytes accessed | tf_op | source)
XLA Modules:
  0.0 76.7 jit_solution(4024632189528749516)
XLA Ops:
  0.7 75.4 %shard_map.109 = bf16[256,384]{1,0:T(8,128)(2,1)S(1)} custom-call(s32[1]{0:T(128)S(6)} %copy.14.len_ref, bf16[7,384]{1,0:T(8,128)(2,1)} %subw.1, bf16[12,384]{1,0:T(8,128)(2,1)} %valw.1, bf16[12,384]{1,0:T(8,128)(2,1)} %gatw.1, bf16[12,384]{1,0:T(8,128)(2,1)} %bitcast.5, f32[320,128]{1,0:T(8,128)} %bitcast.4, f32[31,384]{1,0:T(8,128)} %dk_hbm.1, f32[384]{0:T(512)} %scale.1, ...), custom_call_target="tpu_custom_call" | custom-call | tf_op jit(solution)/shard_map/pallas_call | solution.py:582
  76.0 0.7 copy.13

commit v7 on v6

--- a/solution.py
+++ b/solution.py
@@ -353,6 +353,7 @@
         far_5()
         send_near(3)
         send_near(4)
+        send_x(3)
 
     arrived(mb.at[pl.ds(0, 7)], mb_r)
     total = mb[0]
@@ -376,7 +377,6 @@
     @on(1)
     def _():
         send_near(5)
-        send_x(3)
         send_x(4)
         from_twin(0)
 
@@ -394,8 +394,10 @@
         stacked, sf[...].astype(BF16), preferred_element_type=F32
     ).astype(BF16)
 
-    for i in (2, 1, 3):
-        push(feats.at[mp], ag_s, ag_r, mp=(mp + i) % 4)
+    for half in range(2):
+        rows = feats.at[mp, pl.ds(128 * half, 128)]
+        for i in (2, 1, 3):
+            push(rows, ag_s, ag_r.at[half], mp=(mp + i) % 4)
 
     @on(0)
     def _():
@@ -410,15 +412,16 @@
         send_twin(3)
         send_twin(4)
 
-    arrived(feats.at[pl.ds(0, 3)], ag_r)
-
-    @pl.loop(0, 8, unroll=2)
-    def _(b):
+    def layer_norm(b):
         rows = pl.ds(pl.multiple_of(b * 32, 32), 32)
         wide = jnp.concatenate([feats[g, rows, :] for g in range(4)], axis=1).astype(F32)
         centered = wide - jnp.mean(wide, axis=1, keepdims=True)
         spread = jnp.mean(centered * centered, axis=1, keepdims=True)
         normed[rows, :] = (centered * lax.rsqrt(spread + 1e-05)).astype(BF16)
+
+    for half in range(2):
+        arrived(feats.at[pl.ds(0, 3), pl.ds(0, 128)], ag_r.at[half])
+        pl.loop(4 * half, 4 * half + 4, unroll=2)(layer_norm)
 
     @on(0)
     def _():
@@ -619,7 +622,7 @@
             dma, dma,
             dma, dma,
             dma, dma,
-            dma, dma,
+            dma, dma((2,)),
             dma((2,)), dma((2,)),
             dma, dma,
             dma((7,)), dma((6,)), dma((6,)),

time: 78 us -> 77.8 us (level)
  no operation moved by 1% of the time
where the time goes in v7:
time: 77.8 us; the launch traced here: 77.2 us
  Pallas kernels  75.9 us (98%)
    pallas_call x1, Pallas kernels, shards(): pl.pallas_call(kernel, out_shape=pltpu.VMEM((256, 384), BF16), in_specs=[...  75.9 us

profile of v7, /device:TPU:1, one launch (start us, length us, event | category | flops | bytes accessed | tf_op | source)
XLA Modules:
  0.0 77.2 jit_solution(1415039492127992123)
XLA Ops:
  0.7 75.9 %shard_map.109 = bf16[256,384]{1,0:T(8,128)(2,1)S(1)} custom-call(s32[1]{0:T(128)S(6)} %copy.14.len_ref, bf16[7,384]{1,0:T(8,128)(2,1)} %subw.1, bf16[12,384]{1,0:T(8,128)(2,1)} %valw.1, bf16[12,384]{1,0:T(8,128)(2,1)} %gatw.1, bf16[12,384]{1,0:T(8,128)(2,1)} %bitcast.5, f32[320,128]{1,0:T(8,128)} %bitcast.4, f32[31,384]{1,0:T(8,128)} %dk_hbm.1, f32[384]{0:T(512)} %scale.1, ...), custom_call_target="tpu_custom_call" | custom-call | tf_op jit(solution)/shard_map/pallas_call | solution.py:585
  76.6 0.7 copy.13
